TPU v7x, 32 devices: a whole 2x2x4 slice. The times are simulated.
32 devices in a mesh: req: 8 (over z, y), tp: 4 (over x, core).
Axes of the slice: x: 2, y: 2, z: 4, core: 2. Of those that a mesh axis runs over, the one named last changes fastest.
Arguments:
- queries: bfloat16 [2048, 2048], P('req', 'tp'), may hold values from -160 to 160
- key_rows: bfloat16 [2048, 2048], P('req', 'tp'), may hold values from -6 to 6
- value_rows: bfloat16 [2048, 2048], P('req', 'tp'), may hold values from -6 to 6
- lengths: int32 [8, 4], P('req'), may hold values from 1 to 128, 256 in all within a row
- adapter_ids: int32 [8, 4], P('req'), may hold values from 0 to 7, as said below
- adapter_home: int32 [8], replicated, may hold values from 0 to 7, each once
- adapter_down: bfloat16 [8, 2048, 16], P('req', 'tp'), may hold values from -0.125 to 0.125
- adapter_up: bfloat16 [8, 16, 2048], P('req'), may hold values from -4 to 4
- output_weight: bfloat16 [2048, 2048], P('tp'), may hold values from -0.125 to 0.125
Outputs:
- block_output: bfloat16 [2048, 2048], P('req', 'tp')
Inputs may be any that keep to these rules, and one draw needn't show every extreme that they name: `adapter_ids`: all prompts together name exactly 2 distinct adapters.
All inputs are finite; a program needn't handle non-finite values.
Results may differ from a plain program's by a relative error of at most 0.0055.
Values may be sent and summed in bfloat16 or wider, within the bound.
No kernel may reach another device: no remote copies, remote signals or barrier semaphores. Data moves between devices by JAX's collectives and lax.ppermute only.
A program may use at most 64 MiB of HBM per device.

v0:
```python
import math

import jax
import jax.numpy as jnp
from jax import lax
from jax.sharding import PartitionSpec as P

HD = 128


def segment_rows(length_row, row_total):
    boundary = jnp.cumsum(length_row)
    position = jnp.arange(row_total, dtype=jnp.int32)
    return jnp.sum((position[:, None] >= boundary[None, :]).astype(jnp.int32), axis=1)


def attend(queries, key_rows, value_rows, segment):
    row_total = queries.shape[0]
    head_count = queries.shape[1] // HD
    shaped_q = queries.reshape(row_total, head_count, HD)
    shaped_k = key_rows.reshape(row_total, head_count, HD)
    shaped_v = value_rows.reshape(row_total, head_count, HD)
    scores = jnp.einsum("qhd,khd->hqk", shaped_q, shaped_k, preferred_element_type=jnp.float32) * (
        1.0 / math.sqrt(HD)
    )
    position = jnp.arange(row_total, dtype=jnp.int32)
    allowed = (segment[:, None] == segment[None, :]) & (position[None, :] <= position[:, None])
    masked = jnp.where(allowed[None], scores, -1e30)
    highest = jnp.max(masked, axis=2, keepdims=True)
    exponent = jnp.where(allowed[None], jnp.exp(masked - highest), 0.0)
    weights = (exponent / jnp.sum(exponent, axis=2, keepdims=True)).astype(jnp.bfloat16)
    mixed = jnp.einsum("hqk,khd->qhd", weights, shaped_v, preferred_element_type=jnp.float32)
    return mixed.reshape(row_total, head_count * HD).astype(jnp.bfloat16)


def lowrank_delta(rank_rows, onehot, factor_up):
    row_total, prompts = onehot.shape
    rank_size = rank_rows.shape[1]
    spread = (onehot[:, :, None] * rank_rows[:, None, :]).reshape(row_total, prompts * rank_size)
    upper = factor_up.astype(jnp.float32).reshape(prompts * rank_size, factor_up.shape[2])
    return jnp.dot(spread, upper, precision=lax.Precision.HIGHEST)


def body(
    queries,
    key_rows,
    value_rows,
    lengths,
    adapter_ids,
    adapter_home,
    adapter_down,
    adapter_up,
    output_weight,
):
    row_total = queries.shape[0]
    prompts = lengths.shape[1]
    segment = segment_rows(lengths[0], row_total)
    prompt_ids = adapter_ids[0]
    downs_all, uppers_all = (
        lax.all_gather(adapter_down, "req", axis=0, tiled=True),
        lax.all_gather(adapter_up, "req", axis=0, tiled=True),
    )
    slot_rows = adapter_home[prompt_ids]
    downs = downs_all[slot_rows]
    uppers = uppers_all[slot_rows]
    attended = attend(queries, key_rows, value_rows, segment)
    onehot = (segment[:, None] == jnp.arange(prompts, dtype=jnp.int32)[None, :]).astype(jnp.float32)
    per_prompt = jnp.einsum("ta,sar->str", attended, downs, preferred_element_type=jnp.float32)
    low_local = jnp.einsum("ts,str->tr", onehot, per_prompt, precision=lax.Precision.HIGHEST)
    base_rows = jnp.dot(attended, output_weight, preferred_element_type=jnp.float32)
    partial_rows = base_rows + lowrank_delta(low_local, onehot, uppers)
    summed = lax.psum_scatter(partial_rows, "tp", scatter_dimension=1, tiled=True)
    return summed.astype(jnp.bfloat16)


def solution(mesh):
    return jax.shard_map(
        body,
        mesh=mesh,
        in_specs=(
            P("req", "tp"),
            P("req", "tp"),
            P("req", "tp"),
            P("req", None),
            P("req", None),
            P(),
            P("req", "tp", None),
            P("req", None, None),
            P("tp", None),
        ),
        out_specs=P("req", "tp"),
        check_vma=False,
    )
```

profile of v0, /device:TPU:0, one launch (start us, length us, event | category | flops | bytes accessed | tf_op | source)
XLA Modules:
  0.0 122.9 jit_solution(15670722755668196792)
XLA Ops:
  6.5 0.0 reduce-scatter.2.cloned.1.call-start
  6.5 1.0 reduce-window.8
  7.5 0.1 convert_reduce_fusion
  7.6 0.1 fusion.11
  7.7 0.0 copy-start.7
  7.7 0.0 copy-start.1
  7.8 0.0 copy-start.6
  7.8 0.0 copy-start.4
  7.8 1.6 %fusion.26 = f32[4,256]{1,0:T(4,128)S(1)} fusion(pred[256,256]{0,1:T(8,128)(4,1)S(1)} %fusion.11, bf16[256,512]{1,0:T(8,128)(2,1)} %param.10, bf16[256,512]{1,0:T(8,128)(2,1)} %param.9), kind=kOutput, calls=%fused_computation.39 | convolution fusion | flops 68419840 | bytes 593920 | tf_op jit(solution)/shard_map/sub | solution.py:30
  9.4 0.0 copy-start.5
  9.4 1.3 %fusion.4 = f32[4,256,256]{1,2,0:T(8,128)} fusion(pred[256,256]{0,1:T(8,128)(4,1)S(1)} %fusion.11, bf16[256,512]{1,0:T(8,128)(2,1)S(1)} %copy-done.2, bf16[256,512]{1,0:T(8,128)(2,1)S(1)} %copy-done.3), kind=kOutput, calls=%fused_computation.10 | convolution fusion | flops 67633152 | bytes 1638400 | tf_op jit(solution)/shard_map/qhd,khd->hqk/dot_general | solution.py:23
  10.8 0.6 gather_fusion
  11.4 32.4 %all_gather.6 = bf16[8,512,16]{1,2,0:T(8,128)(2,1)S(1)} all-gather(bf16[1,512,16]{1,2,0:T(8,128)(2,1)S(1)} %copy-done.6), channel_id=1, replica_groups=mesh['req'=8,'tp'=4] {'req'}, dimensions={0}, use_global_device_ids=true | all-gather | bytes 147456 | tf_op jit(solution)/shard_map/all_gather | solution.py:60
  43.8 0.1 copy.35
  44.0 31.2 %all_gather.7 = bf16[8,16,2048]{2,1,0:T(8,128)(2,1)S(1)} all-gather(bf16[1,16,2048]{2,1,0:T(8,128)(2,1)S(1)} %copy-done.5), channel_id=1, replica_groups=mesh['req'=8,'tp'=4] {'req'}, dimensions={0}, use_global_device_ids=true | all-gather | bytes 589824 | tf_op jit(solution)/shard_map/all_gather | solution.py:61
  75.2 0.6 gather_fusion.1
  75.7 0.6 gather_fusion.2
  76.3 2.0 %convolution_convert_fusion = bf16[4,256,128]{1,2,0:T(8,128)(2,1)S(1)} fusion(bf16[256,4,128]{0,2,1:T(8,128)(2,1)S(1)} %bitcast.65, f32[4,256]{1,0:T(4,128)S(1)} %fusion.26, f32[4,256,256]{1,2,0:T(8,128)} %fusion.4, pred[256,256]{0,1:T(8,128)(4,1)S(1)} %fusion.11), kind=kOutput, calls=%fused_computation.11 | convolution fusion | flops 68289792 | bytes 1642496 | tf_op jit(solution)/shard_map/hqk,khd->qhd/dot_general | solution.py:32
  78.3 0.2 fusion.6
  78.5 1.0 convolution_bitcast_fusion
  79.6 2.1 %convolution_add_fusion = f32[256,2048]{1,0:T(8,128)} fusion(f32[256,2048]{1,0:T(8,128)S(1)} %convolution_bitcast_fusion, bf16[256,512]{0,1:T(8,128)(2,1)S(1)} %bitcast.64, bf16[512,2048]{1,0:T(8,128)(2,1)S(1)} %copy-done), kind=kOutput, calls=%fused_computation.5 | convolution fusion | flops 537395200 | bytes 6553600 | tf_op jit(solution)/shard_map/dot_general | solution.py:70
  81.7 0.0 reduce-scatter.2.cloned.1.call-update
  81.7 32.6 %reduce-scatter.2.cloned.1.call-done = f32[256,512]{1,0:T(8,128)} async-done(((f32[256,2048]{1,0:T(8,128)}), f32[256,512]{1,0:T(8,128)}) %reduce-scatter.2.cloned.1.call-update) | async-done | bytes 524304 | tf_op jit(solution)/shard_map/reduce_scatter | solution.py:72
  114.3 1.8 %convert_element_type.32 = bf16[256,512]{1,0:T(8,128)(2,1)} convert(f32[256,512]{1,0:T(8,128)} %reduce-scatter.2.cloned.1.call-done) | non-fusion elementwise | flops 131072 | bytes 786432 | tf_op jit(solution)/shard_map/convert_element_type | solution.py:73
  (16 shorter events, 0.1 us)
Async XLA Ops:
  6.5 73.0 %copy-start = (bf16[512,2048]{1,0:T(8,128)(2,1)S(1)}, bf16[512,2048]{1,0:T(8,128)(2,1)}, u32[]{:S(2)}) copy-start(bf16[512,2048]{1,0:T(8,128)(2,1)} %param.17) | copy-start | bytes 6291460
  6.5 2.9 %copy-start.2 = (bf16[256,512]{1,0:T(8,128)(2,1)S(1)}, bf16[256,512]{1,0:T(8,128)(2,1)}, u32[]{:S(2)}) copy-start(bf16[256,512]{1,0:T(8,128)(2,1)} %param.10) | copy-start | bytes 786436
  6.5 2.9 %copy-start.3 = (bf16[256,512]{1,0:T(8,128)(2,1)S(1)}, bf16[256,512]{1,0:T(8,128)(2,1)}, u32[]{:S(2)}) copy-start(bf16[256,512]{1,0:T(8,128)(2,1)} %param.9) | copy-start | bytes 786436
  6.5 107.8 %reduce-scatter.2.cloned.1.call-start = ((), (), s32[]{:S(2)}) async-start(), calls=%async_computation.1 | async-start | bytes 2621440 | tf_op jit(solution)/shard_map/reduce_scatter | solution.py:72
  7.7 3.0 %copy-start.7 = (s32[1,4]{1,0:T(1,128)S(1)}, s32[1,4]{1,0:T(1,128)}, u32[]{:S(2)}) copy-start(s32[1,4]{1,0:T(1,128)} %param.13) | copy-start | bytes 52
  7.7 3.0 %copy-start.1 = (s32[8]{0:T(128)S(1)}, s32[8]{0:T(128)}, u32[]{:S(2)}) copy-start(s32[8]{0:T(128)} %param.14) | copy-start | bytes 100
  7.8 3.7 %copy-start.6 = (bf16[1,512,16]{1,2,0:T(8,128)(2,1)S(1)}, bf16[1,512,16]{1,2,0:T(8,128)(2,1)}, u32[]{:S(2)}) copy-start(bf16[1,512,16]{1,2,0:T(8,128)(2,1)} %param.15) | copy-start | bytes 49156
  7.8 36.1 %copy-start.4 = (bf16[256,512]{1,0:T(8,128)(2,1)S(1)}, bf16[256,512]{1,0:T(8,128)(2,1)}, u32[]{:S(2)}) copy-start(bf16[256,512]{1,0:T(8,128)(2,1)} %param.11) | copy-start | bytes 786436
  9.4 34.6 %copy-start.5 = (bf16[1,16,2048]{2,1,0:T(8,128)(2,1)S(1)}, bf16[1,16,2048]{2,1,0:T(8,128)(2,1)}, u32[]{:S(2)}) copy-start(bf16[1,16,2048]{2,1,0:T(8,128)(2,1)} %param.16) | copy-start | bytes 196612
Sparse Core Ops, SparseCore 0:
  81.8 32.4 reduce-scatter.1
where the time goes:
time: 123 us
  blocking collectives  63.6 us (52%)
  waiting for transfers between devices  32.6 us (27%)
  between operations  13.5 us (11%)
  matrix products  8.27 us (7%)
  other arithmetic  2.97 us (2%)
  local copies, waits for them, and re-layouts  1.93 us (2%)
    reduce_scatter x1, waiting for transfers between devices, body(): lax.psum_scatter(partial_rows, 'tp', scatter_dimension=1, tiled=True)  32.6 us
    all_gather x1, blocking collectives, body(): lax.all_gather(adapter_down, 'req', axis=0, tiled=True)  32.4 us
    all_gather x1, blocking collectives, body(): lax.all_gather(adapter_up, 'req', axis=0, tiled=True)  31.2 us
  transfers between devices with their start and end apart: 1, of which 1 were waited for; matrix products, arithmetic and copies ran while one was open for 0% of the time, Pallas kernels for 0%

commit v1 on v0

v1 whole, which is shorter than its diff:
```python
import functools
import math

import jax
import jax.numpy as jnp
from jax import lax
from jax.experimental import pallas as pl
from jax.experimental.pallas import tpu as pltpu
from jax.sharding import PartitionSpec as P

HD = 128
VMEM = pl.BlockSpec(memory_space=pltpu.VMEM)
SMEM = pl.BlockSpec(memory_space=pltpu.SMEM)
HBM = pl.BlockSpec(memory_space=pl.ANY)
F32, BF16 = jnp.float32, jnp.bfloat16


def dot(a, b, contract):
    return lax.dot_general(a, b, ((contract[0:1], contract[1:2]), ((), ())), preferred_element_type=F32)


def segment_start(len_ref, position):
    start, boundary = jnp.zeros_like(position), 0
    for s in range(len_ref.shape[1] - 1):
        boundary += len_ref[0, s]
        start = jnp.where(position >= boundary, boundary, start)
    return start


def prompt_mask(len_ref, s, position):
    low = sum((len_ref[0, i] for i in range(s)), jnp.int32(0))
    high = low + len_ref[0, s]
    return (position >= low) & (position < high)


def attend(q, k, v, len_ref, row0):
    rows, keys = q.shape[0], k.shape[0]
    scores = dot(q, k, (1, 1)) * (1.0 / math.sqrt(HD))
    query_at = row0 + lax.broadcasted_iota(jnp.int32, (rows, 1), 0)
    start = segment_start(len_ref, query_at)
    key_at = lax.broadcasted_iota(jnp.int32, (rows, keys), 1)
    masked = jnp.where((key_at >= start) & (key_at <= query_at), scores, -1e30)
    exponent = jnp.exp(masked - jnp.max(masked, axis=1, keepdims=True))
    weights = exponent * (1.0 / jnp.sum(exponent, axis=1, keepdims=True))
    return dot(weights.astype(BF16), v, (1, 0)).astype(BF16)


def attend_kernel(col_far, col_mid, len_ref, q_ref, k_ref, v_ref, w_ref, att_ref, far_ref, mid_ref):
    rows, width = q_ref.shape
    half = rows // 2
    for h in range(width // HD):
        cols = slice(h * HD, (h + 1) * HD)
        for c in range(2):
            att_ref[c * half : (c + 1) * half, cols] = attend(
                q_ref[c * half : (c + 1) * half, cols],
                k_ref[: (c + 1) * half, cols],
                v_ref[: (c + 1) * half, cols],
                len_ref,
                c * half,
            )
    att = att_ref[...]
    part = far_ref.shape[1]
    far_ref[...] = dot(att, w_ref[:, pl.ds(pl.multiple_of(col_far() * part, part), part)], (1, 0)).astype(BF16)
    mid_ref[...] = dot(att, w_ref[:, pl.ds(pl.multiple_of(col_mid() * part, part), part)], (1, 0))


def project_kernel(col_near, col_own, att_ref, w_ref, near_ref, own_ref):
    att = att_ref[...]
    part = near_ref.shape[1]
    near_ref[...] = dot(att, w_ref[:, pl.ds(pl.multiple_of(col_near() * part, part), part)], (1, 0)).astype(BF16)
    own_ref[...] = dot(att, w_ref[:, pl.ds(pl.multiple_of(col_own() * part, part), part)], (1, 0))


def place(ids_ref, home_ref, s):
    return home_ref[ids_ref[0, s]] ^ lax.axis_index("req")


def low_kernel(len_ref, ids_ref, home_ref, att_ref, fac_ref, low_ref):
    rank, rows = low_ref.shape
    prompts = len_ref.shape[1]
    downs = jnp.concatenate([fac_ref[place(ids_ref, home_ref, s), :rank, :] for s in range(prompts)], axis=0)
    every = dot(downs, att_ref[...], (1, 1))
    position = lax.broadcasted_iota(jnp.int32, (rank, rows), 1)
    low = jnp.zeros((rank, rows), F32)
    for s in range(prompts):
        low = jnp.where(prompt_mask(len_ref, s, position), every[s * rank : (s + 1) * rank], low)
    low_ref[...] = low


def final_kernel(len_ref, ids_ref, home_ref, own_ref, near_ref, far_ref, l0, l1, l2, l3, fac_ref, out_ref):
    rank, rows = l0.shape
    prompts = len_ref.shape[1]
    low = (l0[...] + l1[...]) + (l2[...] + l3[...])
    position = lax.broadcasted_iota(jnp.int32, (rank, rows), 1)
    spread = jnp.concatenate([jnp.where(prompt_mask(len_ref, s, position), low, 0.0) for s in range(prompts)], axis=0)
    uppers = jnp.concatenate([fac_ref[place(ids_ref, home_ref, s), rank:, :] for s in range(prompts)], axis=0)
    high = spread.astype(BF16)
    rest = (spread - high.astype(F32)).astype(BF16)
    delta = dot(high, uppers, (0, 0)) + dot(rest, uppers, (0, 0))
    base = own_ref[...] + near_ref[...].astype(F32) + far_ref[...].astype(F32)
    out_ref[...] = (base + delta).astype(BF16)


def swap(array, axis, size, k):
    return lax.ppermute(array, axis, [(i, i ^ k) for i in range(size)])


def body(n_req, n_tp, queries, key_rows, value_rows, lengths, adapter_ids, adapter_home, adapter_down, adapter_up, output_weight):
    rows, width = queries.shape
    part = output_weight.shape[1] // n_tp
    rank = adapter_down.shape[2]
    shape = jax.ShapeDtypeStruct
    col = lambda k: lambda: lax.axis_index("tp") ^ k

    own_up = lax.dynamic_slice_in_dim(adapter_up[0], lax.axis_index("tp") * part, part, 1)
    factors = jnp.concatenate([adapter_down[0].T, own_up], axis=0)[None]
    gathered = GATHER(factors, n_req)

    att, far_part, mid_part = pl.pallas_call(
        functools.partial(attend_kernel, col(3), col(2)),
        in_specs=[SMEM] + [VMEM] * 4,
        out_specs=[VMEM] * 3,
        out_shape=[shape((rows, width), BF16), shape((rows, part), BF16), shape((rows, part), F32)],
        name="attend",
    )(lengths, queries, key_rows, value_rows, output_weight)
    from_near = swap(far_part, "tp", n_tp, 1)
    to_far = (mid_part + from_near.astype(F32)).astype(BF16)
    from_far = swap(to_far, "tp", n_tp, 2)
    near_part, own_part = pl.pallas_call(
        functools.partial(project_kernel, col(1), col(0)),
        in_specs=[VMEM] * 2,
        out_specs=[VMEM] * 2,
        out_shape=[shape((rows, part), BF16), shape((rows, part), F32)],
        name="project",
    )(att, output_weight)
    near = swap(near_part, "tp", n_tp, 1)
    low = pl.pallas_call(
        low_kernel,
        in_specs=[SMEM] * 3 + [VMEM] * 2,
        out_specs=VMEM,
        out_shape=shape((rank, rows), F32),
        name="low",
    )(lengths, adapter_ids, adapter_home, att, gathered)
    lows = [low] + [swap(low, "tp", n_tp, k) for k in (1, 2, 3)]
    return pl.pallas_call(
        final_kernel,
        in_specs=[SMEM] * 3 + [VMEM] * 8,
        out_specs=VMEM,
        out_shape=shape((rows, part), BF16),
        name="final",
    )(lengths, adapter_ids, adapter_home, own_part, near, from_far, *lows, gathered)


def GATHER(block, n_req):
    step = 1
    while step < n_req:
        block = jnp.concatenate([block, swap(block, "req", n_req, step)], axis=0)
        step *= 2
    return block


def solution(mesh):
    return jax.shard_map(
        functools.partial(body, mesh.shape["req"], mesh.shape["tp"]),
        mesh=mesh,
        in_specs=(
            P("req", "tp"),
            P("req", "tp"),
            P("req", "tp"),
            P("req", None),
            P("req", None),
            P(),
            P("req", "tp", None),
            P("req", None, None),
            P("tp", None),
        ),
        out_specs=P("req", "tp"),
        check_vma=False,
    )
```

time: 123 us -> 34.7 us (0.28)
  blocking collectives: 63.6 us -> 0 us
  waiting for transfers between devices: 32.6 us -> 8.17 us
  between operations: 13.5 us -> 0.07 us
  Pallas kernels: 0 us -> 12 us
  starting transfers between devices: 0.01 us -> 10.9 us
  matrix products: 8.27 us -> 0 us
  other arithmetic: 2.97 us -> 1.54 us
    all_gather x2 -> x0, blocking collectives: 63.6 us -> none  [the longest x1 32.4 us: body(): lax.all_gather(adapter_down, 'req', axis=0, tiled=True)]
    reduce_scatter x1 -> x0, waiting for transfers between devices: 32.6 us -> none  [body(): lax.psum_scatter(partial_rows, 'tp', scatter_dimension=1, tiled=True)]
    pallas_call x0 -> x4, Pallas kernels: none -> 12 us  [the longest x1 4.9 us: body(): pl.pallas_call(functools.partial(attend_kernel, col(3), col(2)), in_specs...]
    ppermute x0 -> x9, starting transfers between devices: none -> 10.9 us  [swap(): return lax.ppermute(array, axis, [(i, i ^ k) for i in range(size)])]
    ppermute x0 -> x9, waiting for transfers between devices: none -> 8.17 us  [swap(): return lax.ppermute(array, axis, [(i, i ^ k) for i in range(size)])]
    dot_general x5 -> x0, matrix products: 6.63 us -> none  [the longest x1 2.1 us: body(): jnp.dot(attended, output_weight, preferred_element_type=jnp.float32)]
    gather x3 -> x0, local copies, waits for them, and re-layouts: 1.75 us -> none  [the longest x1 0.64 us: body(): slot_rows = adapter_home[prompt_ids]]
    convert_element_type x2 -> x1, other arithmetic: 1.78 us -> 0.07 us  [body(): to_far = (mid_part + from_near.astype(F32)).astype(BF16)]
  transfers between devices with their start and end apart: 1 -> 9, of which waited for: 1 -> 3; matrix products, arithmetic and copies ran while one was open for 0% -> 2% of each run, Pallas kernels for 0% -> 28%
where the time goes in v1:
time: 34.7 us; the launch traced here: 34.3 us
  Pallas kernels  12 us (35%)
  starting transfers between devices  10.9 us (31%)
  waiting for transfers between devices  8.17 us (24%)
  local copies, waits for them, and re-layouts  1.62 us (5%)
  other arithmetic  1.54 us (4%)
    ppermute x9, starting transfers between devices, swap(): return lax.ppermute(array, axis, [(i, i ^ k) for i in range(size)])  10.9 us
    ppermute x9, waiting for transfers between devices, swap(): return lax.ppermute(array, axis, [(i, i ^ k) for i in range(size)])  8.17 us
    pallas_call x1, Pallas kernels, body(): pl.pallas_call(functools.partial(attend_kernel, col(3), col(2)), in_specs...  4.9 us
    pallas_call x1, Pallas kernels, body(): pl.pallas_call(functools.partial(project_kernel, col(1), col(0)), in_spec...  2.92 us
    pallas_call x1, Pallas kernels, body(): pl.pallas_call(final_kernel, in_specs=[SMEM] * 3 + [VMEM] * 8, out_specs=...  2.38 us
    pallas_call x1, Pallas kernels, body(): pl.pallas_call(low_kernel, in_specs=[SMEM] * 3 + [VMEM] * 2, out_specs=VM...  1.83 us
    unnamed x14, local copies, waits for them, and re-layouts  1.62 us
    concatenate x3, other arithmetic, GATHER(): block = jnp.concatenate([block, swap(block, 'req', n_req, step)], axis=0)  0.75 us
  transfers between devices with their start and end apart: 9, of which 3 were waited for; matrix products, arithmetic and copies ran while one was open for 2% of the time, Pallas kernels for 28%

profile of v1, /device:TPU:0, one launch (start us, length us, event | category | flops | bytes accessed | tf_op | source)
XLA Modules:
  0.0 34.3 jit_solution(8510118845190494377)
XLA Ops:
  0.0 0.8 %copy-done = bf16[1,16,2048]{2,1,0:T(8,128)(2,1)S(1)} copy-done((bf16[1,16,2048]{2,1,0:T(8,128)(2,1)S(1)}, bf16[1,16,2048]{2,1,0:T(8,128)(2,1)}, u32[]{:S(2)}) %copy-start) | copy-done | bytes 65560
  0.8 0.7 %maximum_bitcast_fusion = bf16[1,32,512]{2,1,0:T(8,128)(2,1)S(1)} fusion(bf16[16,512]{1,0:T(8,128)(2,1)S(1)} %dynamic-slice_bitcast_fusion, bf16[16,512]{1,0:T(8,128)(2,1)} %bitcast.7), kind=kLoop, calls=%fused_computation.4 | loop fusion | flops 65536 | bytes 65536 | tf_op jit(solution)/shard_map/broadcast_in_dim | solution.py:116
  1.6 3.0 %collective-permute-start.3 = (bf16[1,32,512]{2,1,0:T(8,128)(2,1)S(1)}, bf16[1,32,512]{2,1,0:T(8,128)(2,1)S(1)}, u32[]{:S(2)}, u32[]{:S(2)}) collective-permute-start(bf16[1,32,512]{2,1,0:T(8,128)(2,1)S(1)} %maximum_bitcast_fusion), channel_id=1, source_target_pairs={{0,4},{4,0},{8,12},{12,8},{16,20},{20,16},{24,28},{28,24},{1,5},{5... | collective-permute-start | bytes 98312 | tf_op jit(solution)/shard_map/ppermute | solution.py:105
  4.5 4.9 %attend.1 = (bf16[256,512]{1,0:T(8,128)(2,1)}, bf16[256,512]{1,0:T(8,128)(2,1)}, f32[256,512]{1,0:T(8,128)}) custom-call(s32[1,4]{1,0:T(1,128)} %len_ref.5, bf16[256,512]{1,0:T(8,128)(2,1)} %q_ref.1, bf16[256,512]{1,0:T(8,128)(2,1)} %k_ref.1, bf16[256,512]{1,0:T(8,128)(2,1)} %v_ref.1, bf16[512,2048]{1,0:T(8,128)(2,1)} %w_ref.3), custom_call_target="tpu_custom_call" | custom-call | tf_op jit(solution)/shard_map/attend/pallas_call | solution.py:119
  9.4 0.0 collective-permute-done.3
  9.5 1.6 %collective-permute-start.4 = (bf16[2,32,512]{2,1,0:T(8,128)(2,1)S(1)}, bf16[2,32,512]{2,1,0:T(8,128)(2,1)S(1)}, u32[]{:S(2)}, u32[]{:S(2)}) collective-permute-start(bf16[2,32,512]{2,1,0:T(8,128)(2,1)S(1)} %pad_maximum_fusion.2), channel_id=1, source_target_pairs={{0,8},{4,12},{8,0},{12,4},{16,24},{20,28},{24,16},{28,20},{1,9},{5... | collective-permute-start | bytes 196616 | tf_op jit(solution)/shard_map/ppermute | solution.py:105
  11.1 2.9 %project.1 = (bf16[256,512]{1,0:T(8,128)(2,1)}, f32[256,512]{1,0:T(8,128)}) custom-call(bf16[256,512]{1,0:T(8,128)(2,1)} %get-tuple-element.10.att_ref, bf16[512,2048]{1,0:T(8,128)(2,1)} %w_ref.3), custom_call_target="tpu_custom_call" | custom-call | tf_op jit(solution)/shard_map/project/pallas_call | solution.py:129
  14.0 0.2 collective-permute-start
  14.2 0.0 collective-permute-done.4
  14.3 2.7 %collective-permute-start.5 = (bf16[4,32,512]{2,1,0:T(8,128)(2,1)S(1)}, bf16[4,32,512]{2,1,0:T(8,128)(2,1)S(1)}, u32[]{:S(2)}, u32[]{:S(2)}) collective-permute-start(bf16[4,32,512]{2,1,0:T(8,128)(2,1)S(1)} %pad_maximum_fusion.1), channel_id=1, source_target_pairs={{0,16},{4,20},{8,24},{12,28},{16,0},{20,4},{24,8},{28,12},{1,17},{... | collective-permute-start | bytes 393224 | tf_op jit(solution)/shard_map/ppermute | solution.py:105
  16.9 0.1 add_convert_fusion
  17.0 1.6 %collective-permute-start.2 = (bf16[256,512]{1,0:T(8,128)(2,1)S(1)}, bf16[256,512]{1,0:T(8,128)(2,1)S(1)}, u32[]{:S(2)}, u32[]{:S(2)}) collective-permute-start(bf16[256,512]{1,0:T(8,128)(2,1)S(1)} %add_convert_fusion), channel_id=1, source_target_pairs={{0,2},{1,3},{2,0},{3,1},{4,6},{5,7},{6,4},{7,5},{8,10},{9,11},{10,... | collective-permute-start | bytes 786440 | tf_op jit(solution)/shard_map/ppermute | solution.py:105
  18.6 5.2 %collective-permute-done.5 = bf16[4,32,512]{2,1,0:T(8,128)(2,1)S(1)} collective-permute-done((bf16[4,32,512]{2,1,0:T(8,128)(2,1)S(1)}, bf16[4,32,512]{2,1,0:T(8,128)(2,1)S(1)}, u32[]{:S(2)}, u32[]{:S(2)}) %collective-permute-start.5) | collective-permute-done | bytes 131104 | tf_op jit(solution)/shard_map/ppermute | solution.py:105
  23.7 0.7 %pad_maximum_fusion.fac_ref = bf16[8,32,512]{2,1,0:T(8,128)(2,1)} fusion(bf16[4,32,512]{2,1,0:T(8,128)(2,1)S(1)} %collective-permute-done.5, bf16[2,32,512]{2,1,0:T(8,128)(2,1)S(1)} %collective-permute-done.4, bf16[1,32,512]{2,1,0:T(8,128)(2,1)S(1)} %collective-permute-done.3, bf16[1,32,512]{2,1,0:T(8,128)(2,1)S(1)} %maximum_bitcast_fusion), kind=kLoop, calls=%fused_computation.1 | loop fusion | flops 393216 | bytes 524288 | tf_op jit(solution)/shard_map/concatenate | solution.py:157
  24.5 1.8 %low.1.l0 = f32[16,256]{1,0:T(8,128)} custom-call(s32[1,4]{1,0:T(1,128)} %len_ref.5, s32[1,4]{1,0:T(1,128)} %ids_ref.3, s32[8]{0:T(128)} %home_ref.3, bf16[256,512]{1,0:T(8,128)(2,1)} %get-tuple-element.10.att_ref, bf16[8,32,512]{2,1,0:T(8,128)(2,1)} %pad_maximum_fusion.fac_ref), custom_call_target="tpu_custom_call" | custom-call | tf_op jit(solution)/shard_map/low/pallas_call | solution.py:137
  26.3 0.9 %collective-permute-start.8 = (f32[16,256]{1,0:T(8,128)}, f32[16,256]{1,0:T(8,128)S(1)}, u32[]{:S(2)}, u32[]{:S(2)}) collective-permute-start(f32[16,256]{1,0:T(8,128)} %low.1.l0), channel_id=1, source_target_pairs={{0,3},{1,2},{2,1},{3,0},{4,7},{5,6},{6,5},{7,4},{8,11},{9,10},{10,... | collective-permute-start | bytes 49160 | tf_op jit(solution)/shard_map/ppermute | solution.py:105
  27.2 0.6 %collective-permute-start.7 = (f32[16,256]{1,0:T(8,128)}, f32[16,256]{1,0:T(8,128)S(1)}, u32[]{:S(2)}, u32[]{:S(2)}) collective-permute-start(f32[16,256]{1,0:T(8,128)} %low.1.l0), channel_id=1, source_target_pairs={{0,2},{1,3},{2,0},{3,1},{4,6},{5,7},{6,4},{7,5},{8,10},{9,11},{10,... | collective-permute-start | bytes 49160 | tf_op jit(solution)/shard_map/ppermute | solution.py:105
  27.8 0.3 collective-permute-start.6
  28.2 1.6 %collective-permute-done.8.l3 = f32[16,256]{1,0:T(8,128)S(1)} collective-permute-done((f32[16,256]{1,0:T(8,128)}, f32[16,256]{1,0:T(8,128)S(1)}, u32[]{:S(2)}, u32[]{:S(2)}) %collective-permute-start.8) | collective-permute-done | bytes 16416 | tf_op jit(solution)/shard_map/ppermute | solution.py:105
  29.8 1.3 %collective-permute-done.7.l2 = f32[16,256]{1,0:T(8,128)S(1)} collective-permute-done((f32[16,256]{1,0:T(8,128)}, f32[16,256]{1,0:T(8,128)S(1)}, u32[]{:S(2)}, u32[]{:S(2)}) %collective-permute-start.7) | collective-permute-done | bytes 16416 | tf_op jit(solution)/shard_map/ppermute | solution.py:105
  31.2 0.5 %copy-done.5 = f32[16,256]{1,0:T(8,128)} copy-done((f32[16,256]{1,0:T(8,128)}, f32[16,256]{1,0:T(8,128)S(1)}, u32[]{:S(2)}) %copy-start.5) | copy-done | bytes 16408
  31.8 0.1 copy-done.2
  31.9 0.1 copy-done.3
  32.0 2.4 %final.1 = bf16[256,512]{1,0:T(8,128)(2,1)} custom-call(s32[1,4]{1,0:T(1,128)} %len_ref.5, s32[1,4]{1,0:T(1,128)} %ids_ref.3, s32[8]{0:T(128)} %home_ref.3, f32[256,512]{1,0:T(8,128)} %get-tuple-element.11.own_ref, bf16[256,512]{1,0:T(8,128)(2,1)} %copy-done.2, bf16[256,512]{1,0:T(8,128)(2,1)} %copy-done.3, f32[16,256]{1,0:T(8,128)} %low.1.l0, ...), custom_call_target="tpu_custom_call" | custom-call | tf_op jit(solution)/shard_map/final/pallas_call | solution.py:145
  (18 shorter events, 0.1 us)
Async XLA Ops:
  0.0 0.8 %copy-start = (bf16[1,16,2048]{2,1,0:T(8,128)(2,1)S(1)}, bf16[1,16,2048]{2,1,0:T(8,128)(2,1)}, u32[]{:S(2)}) copy-start(bf16[1,16,2048]{2,1,0:T(8,128)(2,1)} %param.16) | copy-start | bytes 196612
  1.6 7.9 %collective-permute-start.3 = (bf16[1,32,512]{2,1,0:T(8,128)(2,1)S(1)}, bf16[1,32,512]{2,1,0:T(8,128)(2,1)S(1)}, u32[]{:S(2)}, u32[]{:S(2)}) collective-permute-start(bf16[1,32,512]{2,1,0:T(8,128)(2,1)S(1)} %maximum_bitcast_fusion), channel_id=1, source_target_pairs={{0,4},{4,0},{8,12},{12,8},{16,20},{20,16},{24,28},{28,24},{1,5},{5... | collective-permute-start | bytes 98312 | tf_op jit(solution)/shard_map/ppermute | solution.py:105
  9.4 7.5 %copy-start.1 = (f32[256,512]{1,0:T(8,128)S(1)}, f32[256,512]{1,0:T(8,128)}, u32[]{:S(2)}) copy-start(f32[256,512]{1,0:T(8,128)} %get-tuple-element.13) | copy-start | bytes 1572868
  9.4 7.5 %collective-permute-start.1 = (bf16[256,512]{1,0:T(8,128)(2,1)}, bf16[256,512]{1,0:T(8,128)(2,1)S(1)}, u32[]{:S(2)}, u32[]{:S(2)}) collective-permute-start(bf16[256,512]{1,0:T(8,128)(2,1)} %get-tuple-element.14), channel_id=1, source_target_pairs={{0,1},{1,0},{2,3},{3,2},{4,5},{5,4},{6,7},{7,6},{8,9},{9,8},{10,11... | collective-permute-start | bytes 786440 | tf_op jit(solution)/shard_map/ppermute | solution.py:105
  9.5 4.8 %collective-permute-start.4 = (bf16[2,32,512]{2,1,0:T(8,128)(2,1)S(1)}, bf16[2,32,512]{2,1,0:T(8,128)(2,1)S(1)}, u32[]{:S(2)}, u32[]{:S(2)}) collective-permute-start(bf16[2,32,512]{2,1,0:T(8,128)(2,1)S(1)} %pad_maximum_fusion.2), channel_id=1, source_target_pairs={{0,8},{4,12},{8,0},{12,4},{16,24},{20,28},{24,16},{28,20},{1,9},{5... | collective-permute-start | bytes 196616 | tf_op jit(solution)/shard_map/ppermute | solution.py:105
  14.0 17.1 %collective-permute-start = (bf16[256,512]{1,0:T(8,128)(2,1)}, bf16[256,512]{1,0:T(8,128)(2,1)S(1)}, u32[]{:S(2)}, u32[]{:S(2)}) collective-permute-start(bf16[256,512]{1,0:T(8,128)(2,1)} %get-tuple-element.12), channel_id=1, source_target_pairs={{0,1},{1,0},{2,3},{3,2},{4,5},{5,4},{6,7},{7,6},{8,9},{9,8},{10,11... | collective-permute-start | bytes 786440 | tf_op jit(solution)/shard_map/ppermute | solution.py:105
  14.3 9.5 %collective-permute-start.5 = (bf16[4,32,512]{2,1,0:T(8,128)(2,1)S(1)}, bf16[4,32,512]{2,1,0:T(8,128)(2,1)S(1)}, u32[]{:S(2)}, u32[]{:S(2)}) collective-permute-start(bf16[4,32,512]{2,1,0:T(8,128)(2,1)S(1)} %pad_maximum_fusion.1), channel_id=1, source_target_pairs={{0,16},{4,20},{8,24},{12,28},{16,0},{20,4},{24,8},{28,12},{1,17},{... | collective-permute-start | bytes 393224 | tf_op jit(solution)/shard_map/ppermute | solution.py:105
  17.0 14.2 %collective-permute-start.2 = (bf16[256,512]{1,0:T(8,128)(2,1)S(1)}, bf16[256,512]{1,0:T(8,128)(2,1)S(1)}, u32[]{:S(2)}, u32[]{:S(2)}) collective-permute-start(bf16[256,512]{1,0:T(8,128)(2,1)S(1)} %add_convert_fusion), channel_id=1, source_target_pairs={{0,2},{1,3},{2,0},{3,1},{4,6},{5,7},{6,4},{7,5},{8,10},{9,11},{10,... | collective-permute-start | bytes 786440 | tf_op jit(solution)/shard_map/ppermute | solution.py:105
  26.3 3.5 %collective-permute-start.8 = (f32[16,256]{1,0:T(8,128)}, f32[16,256]{1,0:T(8,128)S(1)}, u32[]{:S(2)}, u32[]{:S(2)}) collective-permute-start(f32[16,256]{1,0:T(8,128)} %low.1.l0), channel_id=1, source_target_pairs={{0,3},{1,2},{2,1},{3,0},{4,7},{5,6},{6,5},{7,4},{8,11},{9,10},{10,... | collective-permute-start | bytes 49160 | tf_op jit(solution)/shard_map/ppermute | solution.py:105
  27.2 3.9 %collective-permute-start.7 = (f32[16,256]{1,0:T(8,128)}, f32[16,256]{1,0:T(8,128)S(1)}, u32[]{:S(2)}, u32[]{:S(2)}) collective-permute-start(f32[16,256]{1,0:T(8,128)} %low.1.l0), channel_id=1, source_target_pairs={{0,2},{1,3},{2,0},{3,1},{4,6},{5,7},{6,4},{7,5},{8,10},{9,11},{10,... | collective-permute-start | bytes 49160 | tf_op jit(solution)/shard_map/ppermute | solution.py:105
  27.8 3.3 %collective-permute-start.6 = (f32[16,256]{1,0:T(8,128)}, f32[16,256]{1,0:T(8,128)S(1)}, u32[]{:S(2)}, u32[]{:S(2)}) collective-permute-start(f32[16,256]{1,0:T(8,128)} %low.1.l0), channel_id=1, source_target_pairs={{0,1},{1,0},{2,3},{3,2},{4,5},{5,4},{6,7},{7,6},{8,9},{9,8},{10,11... | collective-permute-start | bytes 49160 | tf_op jit(solution)/shard_map/ppermute | solution.py:105
  29.8 1.4 %copy-start.4 = (f32[16,256]{1,0:T(8,128)}, f32[16,256]{1,0:T(8,128)S(1)}, u32[]{:S(2)}) copy-start(f32[16,256]{1,0:T(8,128)S(1)} %collective-permute-done.8.l3) | copy-start | bytes 49156
  31.1 0.6 %copy-start.5 = (f32[16,256]{1,0:T(8,128)}, f32[16,256]{1,0:T(8,128)S(1)}, u32[]{:S(2)}) copy-start(f32[16,256]{1,0:T(8,128)S(1)} %collective-permute-done.7.l2) | copy-start | bytes 49156
  31.2 0.6 %copy-start.6 = (f32[16,256]{1,0:T(8,128)}, f32[16,256]{1,0:T(8,128)S(1)}, u32[]{:S(2)}) copy-start(f32[16,256]{1,0:T(8,128)S(1)} %collective-permute-done.6.l1) | copy-start | bytes 49156
  31.2 0.7 %copy-start.2 = (bf16[256,512]{1,0:T(8,128)(2,1)}, bf16[256,512]{1,0:T(8,128)(2,1)S(1)}, u32[]{:S(2)}) copy-start(bf16[256,512]{1,0:T(8,128)(2,1)S(1)} %collective-permute-done.near_ref) | copy-start | bytes 786436
  31.2 0.8 %copy-start.3 = (bf16[256,512]{1,0:T(8,128)(2,1)}, bf16[256,512]{1,0:T(8,128)(2,1)S(1)}, u32[]{:S(2)}) copy-start(bf16[256,512]{1,0:T(8,128)(2,1)S(1)} %collective-permute-done.2.far_ref) | copy-start | bytes 786436

commit v2 on v0

v2 whole, which is shorter than its diff:
```python
import functools
import math

import jax
import jax.numpy as jnp
from jax import lax
from jax.experimental import pallas as pl
from jax.experimental.pallas import tpu as pltpu
from jax.sharding import PartitionSpec as P

HD = 128
VMEM = pl.BlockSpec(memory_space=pltpu.VMEM)
HBM = pl.BlockSpec(memory_space=pltpu.HBM)
F32, BF16 = jnp.float32, jnp.bfloat16


def dot(a, b, contract):
    return lax.dot_general(a, b, ((contract[0:1], contract[1:2]), ((), ())), preferred_element_type=F32)


def attend_kernel(
    hops,
    q_hbm,
    k_hbm,
    v_hbm,
    w_hbm,
    len_hbm,
    ids_hbm,
    home_hbm,
    att_ref,
    place_ref,
    far_ref,
    near_ref,
    mid_ref,
    own_ref,
    q_ref,
    k_ref,
    v_ref,
    w_ref,
    len_ref,
    ids_ref,
    home_ref,
    sems,
):
    rows, width = q_ref.shape
    pairs = (
        (len_hbm, len_ref),
        (ids_hbm, ids_ref),
        (home_hbm, home_ref),
        (q_hbm, q_ref),
        (k_hbm, k_ref),
        (v_hbm, v_ref),
        (w_hbm, w_ref),
    )
    copies = [pltpu.make_async_copy(source, target, sems.at[i]) for i, (source, target) in enumerate(pairs)]
    for copy in copies:
        copy.start()
    for copy in copies[:3]:
        copy.wait()

    me = lax.axis_index("req")
    row_at = lax.broadcasted_iota(jnp.int32, (rows, 1), 0)
    col_at = lax.broadcasted_iota(jnp.int32, place_ref.shape, 1)
    start, boundary = jnp.zeros((rows, 1), jnp.int32), jnp.int32(0)
    place = jnp.zeros(place_ref.shape, jnp.int32)
    for s in range(len_ref.shape[1]):
        distance = home_ref[ids_ref[0, s]] ^ me
        spot = sum((jnp.where((distance & k) != 0, 1 << j, 0) for j, k in enumerate(hops)), jnp.int32(0))
        start = jnp.where(row_at >= boundary, boundary, start)
        place = jnp.where(col_at >= boundary, spot, place)
        boundary += len_ref[0, s]
    place_ref[...] = place

    half = rows // 2
    items = [(h, c * half, (c + 1) * half) for h in range(width // HD) for c in range(2)]
    allowed = {}
    for _, low, high in items[:2]:
        query_at = low + lax.broadcasted_iota(jnp.int32, (half, 1), 0)
        key_at = lax.broadcasted_iota(jnp.int32, (half, high), 1)
        allowed[low] = (key_at >= start[low:high]) & (key_at <= query_at)
    copies[3].wait()
    copies[4].wait()
    scores = [
        dot(q_ref[low:high, h * HD : (h + 1) * HD], k_ref[:high, h * HD : (h + 1) * HD], (1, 1)) for h, low, high in items
    ]
    weights = []
    for score, (h, low, high) in zip(scores, items):
        masked = jnp.where(allowed[low], score * (1.0 / math.sqrt(HD)), -1e30)
        exponent = jnp.exp(masked - jnp.max(masked, axis=1, keepdims=True))
        weights.append((exponent * (1.0 / jnp.sum(exponent, axis=1, keepdims=True))).astype(BF16))
    copies[5].wait()
    mixed = [
        dot(weight, v_ref[:high, h * HD : (h + 1) * HD], (1, 0)).astype(BF16)
        for weight, (h, low, high) in zip(weights, items)
    ]
    for value, (h, low, high) in zip(mixed, items):
        att_ref[low:high, h * HD : (h + 1) * HD] = value

    att = att_ref[...]
    part = far_ref.shape[1]
    mine = lax.axis_index("tp")
    copies[6].wait()
    for k, ref in ((3, far_ref), (2, mid_ref), (1, near_ref), (0, own_ref)):
        block = w_ref[:, pl.ds(pl.multiple_of((mine ^ k) * part, part), part)]
        ref[...] = dot(att, block, (1, 0)).astype(ref.dtype)


def of_prompt(place_ref, rank, blocks):
    row_place = lax.broadcasted_iota(jnp.int32, (blocks * rank, place_ref.shape[1]), 0) // rank
    return row_place == place_ref[0:1, :]


def low_kernel(place_ref, att_ref, held_ref, came_ref, low_ref):
    rank, rows = low_ref.shape
    blocks, _, width = held_ref.shape
    chosen = of_prompt(place_ref, rank, 2 * blocks)
    total = jnp.zeros((rank, rows), F32)
    for n, ref in enumerate((held_ref, came_ref)):
        every = dot(ref[...].reshape(blocks * rank, width), att_ref[...], (1, 1))
        every = jnp.where(chosen[n * blocks * rank : (n + 1) * blocks * rank], every, 0.0)
        total += jnp.sum(every.reshape(blocks, rank, rows), axis=0)
    low_ref[...] = total


def final_kernel(place_ref, own_ref, near_ref, far_ref, low0_ref, low1_ref, held_ref, came_ref, out_ref):
    rank, rows = low0_ref.shape
    blocks, _, part = held_ref.shape
    low = low0_ref[...] + low1_ref[...]
    spread = jnp.where(of_prompt(place_ref, rank, 2 * blocks), jnp.concatenate([low] * (2 * blocks), axis=0), 0.0)
    uppers = jnp.concatenate([ref[...].reshape(blocks * rank, part) for ref in (held_ref, came_ref)], axis=0)
    high = spread.astype(BF16)
    rest = (spread - high.astype(F32)).astype(BF16)
    delta = dot(high, uppers, (0, 0)) + dot(rest, uppers, (0, 0))
    base = own_ref[...] + near_ref[...].astype(F32) + far_ref[...].astype(F32)
    out_ref[...] = (base + delta).astype(BF16)


def swap(array, axis, size, k):
    return lax.ppermute(array, axis, [(i, i ^ k) for i in range(size)])


def call(kernel, name, operands, specs, out, mib, us, scratch=(), place=pltpu.VMEM):
    return pl.pallas_call(
        kernel,
        in_specs=specs,
        out_specs=[VMEM] * len(out),
        out_shape=[place(s, d) for s, d in out],
        scratch_shapes=scratch,
        compiler_params=pltpu.CompilerParams(vmem_limit_bytes=mib << 20),
        cost_estimate=pl.CostEstimate(flops=int(us * 1e9), bytes_accessed=int(us * 3.6e6), transcendentals=0),
        name=name,
    )(*operands)


def body(n_req, n_tp, queries, key_rows, value_rows, lengths, adapter_ids, adapter_home, adapter_down, adapter_up, output_weight):
    rows, width = queries.shape
    part = output_weight.shape[1] // n_tp
    rank = adapter_down.shape[2]
    hops = [n_req >> (j + 1) for j in range(n_req.bit_length() - 1)]
    tie = lax.optimization_barrier

    own_up = lax.dynamic_slice_in_dim(adapter_up[0], lax.axis_index("tp") * part, part, 1)
    held = jnp.concatenate([adapter_down[0].T, own_up], axis=0)[None]
    queries, held = tie((queries, held))
    inputs = [
        pltpu.with_memory_space_constraint(a, pltpu.HBM)
        for a in (queries, key_rows, value_rows, output_weight, lengths, adapter_ids, adapter_home)
    ]
    att, place, far_part, near_part, mid_part, own_part = call(
        functools.partial(attend_kernel, hops),
        "attend",
        inputs,
        [HBM] * 7,
        [((rows, width), BF16), ((8, rows), jnp.int32)] + [((rows, part), BF16)] * 2 + [((rows, part), F32)] * 2,
        16,
        3,
        [pltpu.VMEM(a.shape, a.dtype) for a in inputs[:4]]
        + [pltpu.SMEM(a.shape, a.dtype) for a in inputs[4:]]
        + [pltpu.SemaphoreType.DMA((7,))],
    )
    came = swap(held, "req", n_req, hops[0])
    held, came, far_part, near_part = tie((held, came, far_part, near_part))
    held = jnp.concatenate([held, came], axis=0)
    from_near = swap(far_part, "tp", n_tp, 1)
    near = swap(near_part, "tp", n_tp, 1)
    to_far = (mid_part + from_near.astype(F32)).astype(BF16)
    from_far = swap(to_far, "tp", n_tp, 2)
    for j, k in enumerate(hops[1:-1]):
        came = swap(held, "req", n_req, k)
        if j == 0:
            held, came, _ = tie((held, came, to_far))
        held = jnp.concatenate([held, came], axis=0)
    downs, ups = held[:, :rank], held[:, rank:]
    downs_came = swap(downs, "req", n_req, hops[-1])
    ups_came = swap(ups, "req", n_req, hops[-1])

    (low,) = call(low_kernel, "low", (place, att, downs, downs_came), [VMEM] * 4, [((rank, rows), F32)], 16, 0.3)
    low = low + swap(low, "tp", n_tp, 1)
    (out,) = call(
        final_kernel,
        "final",
        (place, own_part, near, from_far, low, swap(low, "tp", n_tp, 2), ups, ups_came),
        [VMEM] * 8,
        [((rows, part), BF16)],
        24,
        1,
        place=jax.ShapeDtypeStruct,
    )
    return out


def solution(mesh):
    return jax.shard_map(
        functools.partial(body, mesh.shape["req"], mesh.shape["tp"]),
        mesh=mesh,
        in_specs=(
            P("req", "tp"),
            P("req", "tp"),
            P("req", "tp"),
            P("req", None),
            P("req", None),
            P(),
            P("req", "tp", None),
            P("req", None, None),
            P("tp", None),
        ),
        out_specs=P("req", "tp"),
        check_vma=False,
    )
```

time: 123 us -> 24 us (0.20)
  blocking collectives: 63.6 us -> 0 us
  waiting for transfers between devices: 32.6 us -> 6.72 us
  between operations: 13.5 us -> 0.07 us
  starting transfers between devices: 0.01 us -> 11.4 us
  matrix products: 8.27 us -> 0 us
  Pallas kernels: 0 us -> 3.95 us
  other arithmetic: 2.97 us -> 0.8 us
    all_gather x2 -> x0, blocking collectives: 63.6 us -> none  [the longest x1 32.4 us: body(): lax.all_gather(adapter_down, 'req', axis=0, tiled=True)]
    reduce_scatter x1 -> x0, waiting for transfers between devices: 32.6 us -> none  [body(): lax.psum_scatter(partial_rows, 'tp', scatter_dimension=1, tiled=True)]
    ppermute x0 -> x9, starting transfers between devices: none -> 11.4 us  [swap(): return lax.ppermute(array, axis, [(i, i ^ k) for i in range(size)])]
    ppermute x0 -> x9, waiting for transfers between devices: none -> 6.72 us  [swap(): return lax.ppermute(array, axis, [(i, i ^ k) for i in range(size)])]
    dot_general x5 -> x0, matrix products: 6.63 us -> none  [the longest x1 2.1 us: body(): jnp.dot(attended, output_weight, preferred_element_type=jnp.float32)]
    pallas_call x0 -> x3, Pallas kernels: none -> 3.95 us  [call(): pl.pallas_call(kernel, in_specs=specs, out_specs=[VMEM] * len(out), out_s...]
    gather x3 -> x0, local copies, waits for them, and re-layouts: 1.75 us -> none  [the longest x1 0.64 us: body(): slot_rows = adapter_home[prompt_ids]]
    convert_element_type x2 -> x1, other arithmetic: 1.78 us -> 0.07 us  [body(): to_far = (mid_part + from_near.astype(F32)).astype(BF16)]
  transfers between devices with their start and end apart: 1 -> 9, of which waited for: 1 -> 4; matrix products, arithmetic and copies ran while one was open for 0% -> 0% of each run, Pallas kernels for 0% -> 12%
where the time goes in v2:
time: 24 us; the launch traced here: 23.8 us
  starting transfers between devices  11.4 us (48%)
  waiting for transfers between devices  6.72 us (28%)
  Pallas kernels  3.95 us (16%)
  local copies, waits for them, and re-layouts  0.87 us (4%)
  other arithmetic  0.8 us (3%)
    ppermute x9, starting transfers between devices, swap(): return lax.ppermute(array, axis, [(i, i ^ k) for i in range(size)])  11.4 us
    ppermute x9, waiting for transfers between devices, swap(): return lax.ppermute(array, axis, [(i, i ^ k) for i in range(size)])  6.72 us
    pallas_call x3, Pallas kernels, call(): pl.pallas_call(kernel, in_specs=specs, out_specs=[VMEM] * len(out), out_s...  3.95 us
    unnamed x4, local copies, waits for them, and re-layouts  0.85 us
    broadcast_in_dim x1, other arithmetic, body(): held = jnp.concatenate([adapter_down[0].T, own_up], axis=0)[None]  0.72 us
  transfers between devices with their start and end apart: 9, of which 4 were waited for; matrix products, arithmetic and copies ran while one was open for 0% of the time, Pallas kernels for 12%

profile of v2, /device:TPU:0, one launch (start us, length us, event | category | flops | bytes accessed | tf_op | source)
XLA Modules:
  0.0 23.8 jit_solution(8477447697369593565)
XLA Ops:
  0.0 0.8 %copy-done = bf16[1,16,2048]{2,1,0:T(8,128)(2,1)S(1)} copy-done((bf16[1,16,2048]{2,1,0:T(8,128)(2,1)S(1)}, bf16[1,16,2048]{2,1,0:T(8,128)(2,1)}, u32[]{:S(2)}) %copy-start) | copy-done | bytes 65560
  0.8 0.7 %maximum_bitcast_fusion = bf16[1,32,512]{2,1,0:T(8,128)(2,1)S(1)} fusion(bf16[16,512]{1,0:T(8,128)(2,1)S(1)} %dynamic-slice_bitcast_fusion, bf16[16,512]{1,0:T(8,128)(2,1)} %bitcast.7), kind=kLoop, calls=%fused_computation.1 | loop fusion | flops 65536 | bytes 65536 | tf_op jit(solution)/shard_map/broadcast_in_dim | solution.py:163
  1.6 4.0 %collective-permute-start = (bf16[1,32,512]{2,1,0:T(8,128)(2,1)S(1)}, bf16[1,32,512]{2,1,0:T(8,128)(2,1)S(1)}, u32[]{:S(2)}, u32[]{:S(2)}) collective-permute-start(bf16[1,32,512]{2,1,0:T(8,128)(2,1)S(1)} %maximum_bitcast_fusion), channel_id=1, source_target_pairs={{0,16},{4,20},{8,24},{12,28},{16,0},{20,4},{24,8},{28,12},{1,17},{... | collective-permute-start | bytes 98312 | tf_op jit(solution)/shard_map/ppermute | solution.py:139
  5.6 2.6 %attend.1 = (bf16[256,512]{1,0:T(8,128)(2,1)S(1)}, s32[8,256]{1,0:T(8,128)S(1)}, bf16[256,512]{1,0:T(8,128)(2,1)S(1)}, bf16[256,512]{1,0:T(8,128)(2,1)S(1)}, f32...) custom-call(bf16[256,512]{1,0:T(8,128)(2,1)} %q_hbm, bf16[256,512]{1,0:T(8,128)(2,1)} %k_hbm.1, bf16[256,512]{1,0:T(8,128)(2,1)} %v_hbm.1, ...), custom_call_target="tpu_custom_call" | custom-call | flops 3000000000 | bytes 10800000 | tf_op jit(solution)/shard_map/attend/pallas_call | solution.py:143
  8.2 0.0 collective-permute-done
  8.3 0.1 collective-permute-start.2
  8.3 0.5 %collective-permute-start.1 = (bf16[256,512]{1,0:T(8,128)(2,1)S(1)}, bf16[256,512]{1,0:T(8,128)(2,1)S(1)}, u32[]{:S(2)}, u32[]{:S(2)}) collective-permute-start(bf16[256,512]{1,0:T(8,128)(2,1)S(1)} %get-tuple-element.25), channel_id=1, source_target_pairs={{0,1},{1,0},{2,3},{3,2},{4,5},{5,4},{6,7},{7,6},{8,9},{9,8},{10,11... | collective-permute-start | bytes 786440 | tf_op jit(solution)/shard_map/ppermute | solution.py:139
  8.8 1.6 %collective-permute-start.4 = (bf16[2,32,512]{2,1,0:T(8,128)(2,1)S(1)}, bf16[2,32,512]{2,1,0:T(8,128)(2,1)S(1)}, u32[]{:S(2)}, u32[]{:S(2)}) collective-permute-start(bf16[2,32,512]{2,1,0:T(8,128)(2,1)S(1)} %constant_dynamic-update-slice_fusion), channel_id=1, source_target_pairs={{0,8},{4,12},{8,0},{12,4},{16,24},{20,28},{24,16},{28,20},{1,9},{5... | collective-permute-start | bytes 196616 | tf_op jit(solution)/shard_map/ppermute | solution.py:139
  10.4 0.0 collective-permute-done.2
  10.4 0.1 add_convert_fusion
  10.5 1.6 %collective-permute-start.3 = (bf16[256,512]{1,0:T(8,128)(2,1)S(1)}, bf16[256,512]{1,0:T(8,128)(2,1)S(1)}, u32[]{:S(2)}, u32[]{:S(2)}) collective-permute-start(bf16[256,512]{1,0:T(8,128)(2,1)S(1)} %add_convert_fusion), channel_id=1, source_target_pairs={{0,2},{1,3},{2,0},{3,1},{4,6},{5,7},{6,4},{7,5},{8,10},{9,11},{10,... | collective-permute-start | bytes 786440 | tf_op jit(solution)/shard_map/ppermute | solution.py:139
  12.1 1.1 %collective-permute-done.4 = bf16[2,32,512]{2,1,0:T(8,128)(2,1)S(1)} collective-permute-done((bf16[2,32,512]{2,1,0:T(8,128)(2,1)S(1)}, bf16[2,32,512]{2,1,0:T(8,128)(2,1)S(1)}, u32[]{:S(2)}, u32[]{:S(2)}) %collective-permute-start.4) | collective-permute-done | bytes 65568 | tf_op jit(solution)/shard_map/ppermute | solution.py:139
  13.1 1.6 %collective-permute-start.5 = (bf16[4,16,512]{2,1,0:T(8,128)(2,1)S(1)}, bf16[4,16,512]{2,1,0:T(8,128)(2,1)S(1)}, u32[]{:S(2)}, u32[]{:S(2)}) collective-permute-start(bf16[4,16,512]{2,1,0:T(8,128)(2,1)S(1)} %get-tuple-element.34.held_ref), channel_id=1, source_target_pairs={{0,4},{4,0},{8,12},{12,8},{16,20},{20,16},{24,28},{28,24},{1,5},{5... | collective-permute-start | bytes 196616 | tf_op jit(solution)/shard_map/ppermute | solution.py:139
  14.7 0.5 %collective-permute-start.8 = (bf16[4,16,512]{2,1,0:T(8,128)(2,1)S(1)}, bf16[4,16,512]{2,1,0:T(8,128)(2,1)S(1)}, u32[]{:S(2)}, u32[]{:S(2)}) collective-permute-start(bf16[4,16,512]{2,1,0:T(8,128)(2,1)S(1)} %get-tuple-element.33.held_ref), channel_id=1, source_target_pairs={{0,4},{4,0},{8,12},{12,8},{16,20},{20,16},{24,28},{28,24},{1,5},{5... | collective-permute-start | bytes 196616 | tf_op jit(solution)/shard_map/ppermute | solution.py:139
  15.2 2.2 %collective-permute-done.5.came_ref = bf16[4,16,512]{2,1,0:T(8,128)(2,1)S(1)} collective-permute-done((bf16[4,16,512]{2,1,0:T(8,128)(2,1)S(1)}, bf16[4,16,512]{2,1,0:T(8,128)(2,1)S(1)}, u32[]{:S(2)}, u32[]{:S(2)}) %collective-permute-start.5) | collective-permute-done | bytes 65568 | tf_op jit(solution)/shard_map/ppermute | solution.py:139
  17.5 0.3 %low.1 = f32[16,256]{1,0:T(8,128)S(1)} custom-call(s32[8,256]{1,0:T(8,128)S(1)} %get-tuple-element.20.place_ref, bf16[256,512]{1,0:T(8,128)(2,1)S(1)} %get-tuple-element.28.att_ref, bf16[4,16,512]{2,1,0:T(8,128)(2,1)S(1)} %get-tuple-element.34.held_ref, bf16[4,16,512]{2,1,0:T(8,128)(2,1)S(1)} %collective-permute-done.5.came_ref), custom_call_target="tpu_custom_call" | custom-call | flops 300000000 | bytes 1080000 | tf_op jit(solution)/shard_map/low/pallas_call | solution.py:143
  17.8 0.1 collective-permute-start.6
  17.8 1.2 %collective-permute-done.6 = f32[16,256]{1,0:T(8,128)S(1)} collective-permute-done((f32[16,256]{1,0:T(8,128)S(1)}, f32[16,256]{1,0:T(8,128)S(1)}, u32[]{:S(2)}, u32[]{:S(2)}) %collective-permute-start.6) | collective-permute-done | bytes 16416 | tf_op jit(solution)/shard_map/ppermute | solution.py:139
  19.0 1.5 %collective-permute-start.7 = (f32[16,256]{1,0:T(8,128)S(1)}, f32[16,256]{1,0:T(8,128)S(1)}, u32[]{:S(2)}, u32[]{:S(2)}) collective-permute-start(f32[16,256]{1,0:T(8,128)S(1)} %add.11.low0_ref), channel_id=1, source_target_pairs={{0,2},{1,3},{2,0},{3,1},{4,6},{5,7},{6,4},{7,5},{8,10},{9,11},{10,... | collective-permute-start | bytes 49160 | tf_op jit(solution)/shard_map/ppermute | solution.py:139
  20.5 0.0 collective-permute-done.1.near_ref
  20.5 0.0 collective-permute-done.8.came_ref
  20.5 2.2 %collective-permute-done.7.low1_ref = f32[16,256]{1,0:T(8,128)S(1)} collective-permute-done((f32[16,256]{1,0:T(8,128)S(1)}, f32[16,256]{1,0:T(8,128)S(1)}, u32[]{:S(2)}, u32[]{:S(2)}) %collective-permute-start.7) | collective-permute-done | bytes 16416 | tf_op jit(solution)/shard_map/ppermute | solution.py:139
  22.7 0.0 collective-permute-done.3.far_ref
  22.7 1.0 %final.1 = bf16[256,512]{1,0:T(8,128)(2,1)} custom-call(s32[8,256]{1,0:T(8,128)S(1)} %get-tuple-element.20.place_ref, f32[256,512]{1,0:T(8,128)S(1)} %get-tuple-element.21.own_ref, bf16[256,512]{1,0:T(8,128)(2,1)S(1)} %collective-permute-done.1.near_ref, bf16[256,512]{1,0:T(8,128)(2,1)S(1)} %collective-permute-done.3.far_ref, f32[16,256]{1,0:T(8,128)S(1)} %add.11.low0_ref, ...), custom_call_target="tpu_custom_call" | custom-call | flops 1000000000 | bytes 3600000 | tf_op jit(solution)/shard_map/final/pallas_call | solution.py:143
  (8 shorter events, 0.0 us)
Async XLA Ops:
  0.0 0.8 %copy-start = (bf16[1,16,2048]{2,1,0:T(8,128)(2,1)S(1)}, bf16[1,16,2048]{2,1,0:T(8,128)(2,1)}, u32[]{:S(2)}) copy-start(bf16[1,16,2048]{2,1,0:T(8,128)(2,1)} %param.16) | copy-start | bytes 196612
  1.6 6.7 %collective-permute-start = (bf16[1,32,512]{2,1,0:T(8,128)(2,1)S(1)}, bf16[1,32,512]{2,1,0:T(8,128)(2,1)S(1)}, u32[]{:S(2)}, u32[]{:S(2)}) collective-permute-start(bf16[1,32,512]{2,1,0:T(8,128)(2,1)S(1)} %maximum_bitcast_fusion), channel_id=1, source_target_pairs={{0,16},{4,20},{8,24},{12,28},{16,0},{20,4},{24,8},{28,12},{1,17},{... | collective-permute-start | bytes 98312 | tf_op jit(solution)/shard_map/ppermute | solution.py:139
  8.3 2.2 %collective-permute-start.2 = (bf16[256,512]{1,0:T(8,128)(2,1)S(1)}, bf16[256,512]{1,0:T(8,128)(2,1)S(1)}, u32[]{:S(2)}, u32[]{:S(2)}) collective-permute-start(bf16[256,512]{1,0:T(8,128)(2,1)S(1)} %get-tuple-element.27), channel_id=1, source_target_pairs={{0,1},{1,0},{2,3},{3,2},{4,5},{5,4},{6,7},{7,6},{8,9},{9,8},{10,11... | collective-permute-start | bytes 786440 | tf_op jit(solution)/shard_map/ppermute | solution.py:139
  8.3 12.2 %collective-permute-start.1 = (bf16[256,512]{1,0:T(8,128)(2,1)S(1)}, bf16[256,512]{1,0:T(8,128)(2,1)S(1)}, u32[]{:S(2)}, u32[]{:S(2)}) collective-permute-start(bf16[256,512]{1,0:T(8,128)(2,1)S(1)} %get-tuple-element.25), channel_id=1, source_target_pairs={{0,1},{1,0},{2,3},{3,2},{4,5},{5,4},{6,7},{7,6},{8,9},{9,8},{10,11... | collective-permute-start | bytes 786440 | tf_op jit(solution)/shard_map/ppermute | solution.py:139
  8.8 4.3 %collective-permute-start.4 = (bf16[2,32,512]{2,1,0:T(8,128)(2,1)S(1)}, bf16[2,32,512]{2,1,0:T(8,128)(2,1)S(1)}, u32[]{:S(2)}, u32[]{:S(2)}) collective-permute-start(bf16[2,32,512]{2,1,0:T(8,128)(2,1)S(1)} %constant_dynamic-update-slice_fusion), channel_id=1, source_target_pairs={{0,8},{4,12},{8,0},{12,4},{16,24},{20,28},{24,16},{28,20},{1,9},{5... | collective-permute-start | bytes 196616 | tf_op jit(solution)/shard_map/ppermute | solution.py:139
  10.5 12.2 %collective-permute-start.3 = (bf16[256,512]{1,0:T(8,128)(2,1)S(1)}, bf16[256,512]{1,0:T(8,128)(2,1)S(1)}, u32[]{:S(2)}, u32[]{:S(2)}) collective-permute-start(bf16[256,512]{1,0:T(8,128)(2,1)S(1)} %add_convert_fusion), channel_id=1, source_target_pairs={{0,2},{1,3},{2,0},{3,1},{4,6},{5,7},{6,4},{7,5},{8,10},{9,11},{10,... | collective-permute-start | bytes 786440 | tf_op jit(solution)/shard_map/ppermute | solution.py:139
  13.1 4.3 %collective-permute-start.5 = (bf16[4,16,512]{2,1,0:T(8,128)(2,1)S(1)}, bf16[4,16,512]{2,1,0:T(8,128)(2,1)S(1)}, u32[]{:S(2)}, u32[]{:S(2)}) collective-permute-start(bf16[4,16,512]{2,1,0:T(8,128)(2,1)S(1)} %get-tuple-element.34.held_ref), channel_id=1, source_target_pairs={{0,4},{4,0},{8,12},{12,8},{16,20},{20,16},{24,28},{28,24},{1,5},{5... | collective-permute-start | bytes 196616 | tf_op jit(solution)/shard_map/ppermute | solution.py:139
  14.7 5.8 %collective-permute-start.8 = (bf16[4,16,512]{2,1,0:T(8,128)(2,1)S(1)}, bf16[4,16,512]{2,1,0:T(8,128)(2,1)S(1)}, u32[]{:S(2)}, u32[]{:S(2)}) collective-permute-start(bf16[4,16,512]{2,1,0:T(8,128)(2,1)S(1)} %get-tuple-element.33.held_ref), channel_id=1, source_target_pairs={{0,4},{4,0},{8,12},{12,8},{16,20},{20,16},{24,28},{28,24},{1,5},{5... | collective-permute-start | bytes 196616 | tf_op jit(solution)/shard_map/ppermute | solution.py:139
  17.8 1.2 %collective-permute-start.6 = (f32[16,256]{1,0:T(8,128)S(1)}, f32[16,256]{1,0:T(8,128)S(1)}, u32[]{:S(2)}, u32[]{:S(2)}) collective-permute-start(f32[16,256]{1,0:T(8,128)S(1)} %low.1), channel_id=1, source_target_pairs={{0,1},{1,0},{2,3},{3,2},{4,5},{5,4},{6,7},{7,6},{8,9},{9,8},{10,11... | collective-permute-start | bytes 49160 | tf_op jit(solution)/shard_map/ppermute | solution.py:139
  19.0 3.7 %collective-permute-start.7 = (f32[16,256]{1,0:T(8,128)S(1)}, f32[16,256]{1,0:T(8,128)S(1)}, u32[]{:S(2)}, u32[]{:S(2)}) collective-permute-start(f32[16,256]{1,0:T(8,128)S(1)} %add.11.low0_ref), channel_id=1, source_target_pairs={{0,2},{1,3},{2,0},{3,1},{4,6},{5,7},{6,4},{7,5},{8,10},{9,11},{10,... | collective-permute-start | bytes 49160 | tf_op jit(solution)/shard_map/ppermute | solution.py:139

commit v3 on v2

--- a/solution.py
+++ b/solution.py
@@ -199,7 +199,7 @@
     (out,) = call(
         final_kernel,
         "final",
-        (place, own_part, near, from_far, low, swap(low, "tp", n_tp, 2), ups, ups_came),
+        (place, own_part, near, from_far, low, swap(low, "tp", n_tp, 3), ups, ups_came),
         [VMEM] * 8,
         [((rows, part), BF16)],
         24,

time: 24 us -> 23.5 us (0.979)
  waiting for transfers between devices: 6.72 us -> 6.38 us
    ppermute x9, waiting for transfers between devices: 6.72 us -> 6.38 us  [swap(): return lax.ppermute(array, axis, [(i, i ^ k) for i in range(size)])]
  transfers between devices with their start and end apart: 9 -> 9, of which waited for: 4 -> 4; matrix products, arithmetic and copies ran while one was open for 0% -> 0% of each run, Pallas kernels for 12% -> 13%
where the time goes in v3:
time: 23.5 us; the launch traced here: 23.2 us
  starting transfers between devices  11.2 us (48%)
  waiting for transfers between devices  6.38 us (27%)
  Pallas kernels  3.95 us (17%)
  local copies, waits for them, and re-layouts  0.87 us (4%)
  other arithmetic  0.8 us (3%)
    ppermute x9, starting transfers between devices, swap(): return lax.ppermute(array, axis, [(i, i ^ k) for i in range(size)])  11.2 us
    ppermute x9, waiting for transfers between devices, swap(): return lax.ppermute(array, axis, [(i, i ^ k) for i in range(size)])  6.38 us
    pallas_call x3, Pallas kernels, call(): pl.pallas_call(kernel, in_specs=specs, out_specs=[VMEM] * len(out), out_s...  3.95 us
    unnamed x4, local copies, waits for them, and re-layouts  0.85 us
    broadcast_in_dim x1, other arithmetic, body(): held = jnp.concatenate([adapter_down[0].T, own_up], axis=0)[None]  0.72 us
  transfers between devices with their start and end apart: 9, of which 4 were waited for; matrix products, arithmetic and copies ran while one was open for 0% of the time, Pallas kernels for 13%

profile of v3, /device:TPU:0, one launch (start us, length us, event | category | flops | bytes accessed | tf_op | source)
XLA Modules:
  0.0 23.2 jit_solution(10043644640755579059)
XLA Ops:
  0.0 0.8 %copy-done = bf16[1,16,2048]{2,1,0:T(8,128)(2,1)S(1)} copy-done((bf16[1,16,2048]{2,1,0:T(8,128)(2,1)S(1)}, bf16[1,16,2048]{2,1,0:T(8,128)(2,1)}, u32[]{:S(2)}) %copy-start) | copy-done | bytes 65560
  0.8 0.7 %maximum_bitcast_fusion = bf16[1,32,512]{2,1,0:T(8,128)(2,1)S(1)} fusion(bf16[16,512]{1,0:T(8,128)(2,1)S(1)} %dynamic-slice_bitcast_fusion, bf16[16,512]{1,0:T(8,128)(2,1)} %bitcast.7), kind=kLoop, calls=%fused_computation.1 | loop fusion | flops 65536 | bytes 65536 | tf_op jit(solution)/shard_map/broadcast_in_dim | solution.py:163
  1.6 4.0 %collective-permute-start = (bf16[1,32,512]{2,1,0:T(8,128)(2,1)S(1)}, bf16[1,32,512]{2,1,0:T(8,128)(2,1)S(1)}, u32[]{:S(2)}, u32[]{:S(2)}) collective-permute-start(bf16[1,32,512]{2,1,0:T(8,128)(2,1)S(1)} %maximum_bitcast_fusion), channel_id=1, source_target_pairs={{0,16},{4,20},{8,24},{12,28},{16,0},{20,4},{24,8},{28,12},{1,17},{... | collective-permute-start | bytes 98312 | tf_op jit(solution)/shard_map/ppermute | solution.py:139
  5.6 2.6 %attend.1 = (bf16[256,512]{1,0:T(8,128)(2,1)S(1)}, s32[8,256]{1,0:T(8,128)S(1)}, bf16[256,512]{1,0:T(8,128)(2,1)S(1)}, bf16[256,512]{1,0:T(8,128)(2,1)S(1)}, f32...) custom-call(bf16[256,512]{1,0:T(8,128)(2,1)} %q_hbm, bf16[256,512]{1,0:T(8,128)(2,1)} %k_hbm.1, bf16[256,512]{1,0:T(8,128)(2,1)} %v_hbm.1, ...), custom_call_target="tpu_custom_call" | custom-call | flops 3000000000 | bytes 10800000 | tf_op jit(solution)/shard_map/attend/pallas_call | solution.py:143
  8.2 0.0 collective-permute-done
  8.3 0.1 collective-permute-start.2
  8.3 0.5 %collective-permute-start.1 = (bf16[256,512]{1,0:T(8,128)(2,1)S(1)}, bf16[256,512]{1,0:T(8,128)(2,1)S(1)}, u32[]{:S(2)}, u32[]{:S(2)}) collective-permute-start(bf16[256,512]{1,0:T(8,128)(2,1)S(1)} %get-tuple-element.25), channel_id=1, source_target_pairs={{0,1},{1,0},{2,3},{3,2},{4,5},{5,4},{6,7},{7,6},{8,9},{9,8},{10,11... | collective-permute-start | bytes 786440 | tf_op jit(solution)/shard_map/ppermute | solution.py:139
  8.8 1.6 %collective-permute-start.4 = (bf16[2,32,512]{2,1,0:T(8,128)(2,1)S(1)}, bf16[2,32,512]{2,1,0:T(8,128)(2,1)S(1)}, u32[]{:S(2)}, u32[]{:S(2)}) collective-permute-start(bf16[2,32,512]{2,1,0:T(8,128)(2,1)S(1)} %constant_dynamic-update-slice_fusion), channel_id=1, source_target_pairs={{0,8},{4,12},{8,0},{12,4},{16,24},{20,28},{24,16},{28,20},{1,9},{5... | collective-permute-start | bytes 196616 | tf_op jit(solution)/shard_map/ppermute | solution.py:139
  10.4 0.0 collective-permute-done.2
  10.4 0.1 add_convert_fusion
  10.5 1.6 %collective-permute-start.3 = (bf16[256,512]{1,0:T(8,128)(2,1)S(1)}, bf16[256,512]{1,0:T(8,128)(2,1)S(1)}, u32[]{:S(2)}, u32[]{:S(2)}) collective-permute-start(bf16[256,512]{1,0:T(8,128)(2,1)S(1)} %add_convert_fusion), channel_id=1, source_target_pairs={{0,2},{1,3},{2,0},{3,1},{4,6},{5,7},{6,4},{7,5},{8,10},{9,11},{10,... | collective-permute-start | bytes 786440 | tf_op jit(solution)/shard_map/ppermute | solution.py:139
  12.1 1.1 %collective-permute-done.4 = bf16[2,32,512]{2,1,0:T(8,128)(2,1)S(1)} collective-permute-done((bf16[2,32,512]{2,1,0:T(8,128)(2,1)S(1)}, bf16[2,32,512]{2,1,0:T(8,128)(2,1)S(1)}, u32[]{:S(2)}, u32[]{:S(2)}) %collective-permute-start.4) | collective-permute-done | bytes 65568 | tf_op jit(solution)/shard_map/ppermute | solution.py:139
  13.1 1.6 %collective-permute-start.5 = (bf16[4,16,512]{2,1,0:T(8,128)(2,1)S(1)}, bf16[4,16,512]{2,1,0:T(8,128)(2,1)S(1)}, u32[]{:S(2)}, u32[]{:S(2)}) collective-permute-start(bf16[4,16,512]{2,1,0:T(8,128)(2,1)S(1)} %get-tuple-element.34.held_ref), channel_id=1, source_target_pairs={{0,4},{4,0},{8,12},{12,8},{16,20},{20,16},{24,28},{28,24},{1,5},{5... | collective-permute-start | bytes 196616 | tf_op jit(solution)/shard_map/ppermute | solution.py:139
  14.7 0.5 %collective-permute-start.8 = (bf16[4,16,512]{2,1,0:T(8,128)(2,1)S(1)}, bf16[4,16,512]{2,1,0:T(8,128)(2,1)S(1)}, u32[]{:S(2)}, u32[]{:S(2)}) collective-permute-start(bf16[4,16,512]{2,1,0:T(8,128)(2,1)S(1)} %get-tuple-element.33.held_ref), channel_id=1, source_target_pairs={{0,4},{4,0},{8,12},{12,8},{16,20},{20,16},{24,28},{28,24},{1,5},{5... | collective-permute-start | bytes 196616 | tf_op jit(solution)/shard_map/ppermute | solution.py:139
  15.2 2.2 %collective-permute-done.5.came_ref = bf16[4,16,512]{2,1,0:T(8,128)(2,1)S(1)} collective-permute-done((bf16[4,16,512]{2,1,0:T(8,128)(2,1)S(1)}, bf16[4,16,512]{2,1,0:T(8,128)(2,1)S(1)}, u32[]{:S(2)}, u32[]{:S(2)}) %collective-permute-start.5) | collective-permute-done | bytes 65568 | tf_op jit(solution)/shard_map/ppermute | solution.py:139
  17.5 0.3 %low.1 = f32[16,256]{1,0:T(8,128)S(1)} custom-call(s32[8,256]{1,0:T(8,128)S(1)} %get-tuple-element.20.place_ref, bf16[256,512]{1,0:T(8,128)(2,1)S(1)} %get-tuple-element.28.att_ref, bf16[4,16,512]{2,1,0:T(8,128)(2,1)S(1)} %get-tuple-element.34.held_ref, bf16[4,16,512]{2,1,0:T(8,128)(2,1)S(1)} %collective-permute-done.5.came_ref), custom_call_target="tpu_custom_call" | custom-call | flops 300000000 | bytes 1080000 | tf_op jit(solution)/shard_map/low/pallas_call | solution.py:143
  17.8 0.1 collective-permute-start.6
  17.8 1.2 %collective-permute-done.6 = f32[16,256]{1,0:T(8,128)S(1)} collective-permute-done((f32[16,256]{1,0:T(8,128)S(1)}, f32[16,256]{1,0:T(8,128)S(1)}, u32[]{:S(2)}, u32[]{:S(2)}) %collective-permute-start.6) | collective-permute-done | bytes 16416 | tf_op jit(solution)/shard_map/ppermute | solution.py:139
  19.0 1.3 %collective-permute-start.7 = (f32[16,256]{1,0:T(8,128)S(1)}, f32[16,256]{1,0:T(8,128)S(1)}, u32[]{:S(2)}, u32[]{:S(2)}) collective-permute-start(f32[16,256]{1,0:T(8,128)S(1)} %add.11.low0_ref), channel_id=1, source_target_pairs={{0,3},{1,2},{2,1},{3,0},{4,7},{5,6},{6,5},{7,4},{8,11},{9,10},{10,... | collective-permute-start | bytes 49160 | tf_op jit(solution)/shard_map/ppermute | solution.py:139
  20.3 0.0 collective-permute-done.1.near_ref
  20.3 0.0 collective-permute-done.8.came_ref
  20.3 1.9 %collective-permute-done.7.low1_ref = f32[16,256]{1,0:T(8,128)S(1)} collective-permute-done((f32[16,256]{1,0:T(8,128)S(1)}, f32[16,256]{1,0:T(8,128)S(1)}, u32[]{:S(2)}, u32[]{:S(2)}) %collective-permute-start.7) | collective-permute-done | bytes 16416 | tf_op jit(solution)/shard_map/ppermute | solution.py:139
  22.2 0.0 collective-permute-done.3.far_ref
  22.2 1.0 %final.1 = bf16[256,512]{1,0:T(8,128)(2,1)} custom-call(s32[8,256]{1,0:T(8,128)S(1)} %get-tuple-element.20.place_ref, f32[256,512]{1,0:T(8,128)S(1)} %get-tuple-element.21.own_ref, bf16[256,512]{1,0:T(8,128)(2,1)S(1)} %collective-permute-done.1.near_ref, bf16[256,512]{1,0:T(8,128)(2,1)S(1)} %collective-permute-done.3.far_ref, f32[16,256]{1,0:T(8,128)S(1)} %add.11.low0_ref, ...), custom_call_target="tpu_custom_call" | custom-call | flops 1000000000 | bytes 3600000 | tf_op jit(solution)/shard_map/final/pallas_call | solution.py:143
  (8 shorter events, 0.0 us)
Async XLA Ops:
  0.0 0.8 %copy-start = (bf16[1,16,2048]{2,1,0:T(8,128)(2,1)S(1)}, bf16[1,16,2048]{2,1,0:T(8,128)(2,1)}, u32[]{:S(2)}) copy-start(bf16[1,16,2048]{2,1,0:T(8,128)(2,1)} %param.16) | copy-start | bytes 196612
  1.6 6.7 %collective-permute-start = (bf16[1,32,512]{2,1,0:T(8,128)(2,1)S(1)}, bf16[1,32,512]{2,1,0:T(8,128)(2,1)S(1)}, u32[]{:S(2)}, u32[]{:S(2)}) collective-permute-start(bf16[1,32,512]{2,1,0:T(8,128)(2,1)S(1)} %maximum_bitcast_fusion), channel_id=1, source_target_pairs={{0,16},{4,20},{8,24},{12,28},{16,0},{20,4},{24,8},{28,12},{1,17},{... | collective-permute-start | bytes 98312 | tf_op jit(solution)/shard_map/ppermute | solution.py:139
  8.3 2.2 %collective-permute-start.2 = (bf16[256,512]{1,0:T(8,128)(2,1)S(1)}, bf16[256,512]{1,0:T(8,128)(2,1)S(1)}, u32[]{:S(2)}, u32[]{:S(2)}) collective-permute-start(bf16[256,512]{1,0:T(8,128)(2,1)S(1)} %get-tuple-element.27), channel_id=1, source_target_pairs={{0,1},{1,0},{2,3},{3,2},{4,5},{5,4},{6,7},{7,6},{8,9},{9,8},{10,11... | collective-permute-start | bytes 786440 | tf_op jit(solution)/shard_map/ppermute | solution.py:139
  8.3 11.9 %collective-permute-start.1 = (bf16[256,512]{1,0:T(8,128)(2,1)S(1)}, bf16[256,512]{1,0:T(8,128)(2,1)S(1)}, u32[]{:S(2)}, u32[]{:S(2)}) collective-permute-start(bf16[256,512]{1,0:T(8,128)(2,1)S(1)} %get-tuple-element.25), channel_id=1, source_target_pairs={{0,1},{1,0},{2,3},{3,2},{4,5},{5,4},{6,7},{7,6},{8,9},{9,8},{10,11... | collective-permute-start | bytes 786440 | tf_op jit(solution)/shard_map/ppermute | solution.py:139
  8.8 4.3 %collective-permute-start.4 = (bf16[2,32,512]{2,1,0:T(8,128)(2,1)S(1)}, bf16[2,32,512]{2,1,0:T(8,128)(2,1)S(1)}, u32[]{:S(2)}, u32[]{:S(2)}) collective-permute-start(bf16[2,32,512]{2,1,0:T(8,128)(2,1)S(1)} %constant_dynamic-update-slice_fusion), channel_id=1, source_target_pairs={{0,8},{4,12},{8,0},{12,4},{16,24},{20,28},{24,16},{28,20},{1,9},{5... | collective-permute-start | bytes 196616 | tf_op jit(solution)/shard_map/ppermute | solution.py:139
  10.5 11.7 %collective-permute-start.3 = (bf16[256,512]{1,0:T(8,128)(2,1)S(1)}, bf16[256,512]{1,0:T(8,128)(2,1)S(1)}, u32[]{:S(2)}, u32[]{:S(2)}) collective-permute-start(bf16[256,512]{1,0:T(8,128)(2,1)S(1)} %add_convert_fusion), channel_id=1, source_target_pairs={{0,2},{1,3},{2,0},{3,1},{4,6},{5,7},{6,4},{7,5},{8,10},{9,11},{10,... | collective-permute-start | bytes 786440 | tf_op jit(solution)/shard_map/ppermute | solution.py:139
  13.1 4.3 %collective-permute-start.5 = (bf16[4,16,512]{2,1,0:T(8,128)(2,1)S(1)}, bf16[4,16,512]{2,1,0:T(8,128)(2,1)S(1)}, u32[]{:S(2)}, u32[]{:S(2)}) collective-permute-start(bf16[4,16,512]{2,1,0:T(8,128)(2,1)S(1)} %get-tuple-element.34.held_ref), channel_id=1, source_target_pairs={{0,4},{4,0},{8,12},{12,8},{16,20},{20,16},{24,28},{28,24},{1,5},{5... | collective-permute-start | bytes 196616 | tf_op jit(solution)/shard_map/ppermute | solution.py:139
  14.7 5.5 %collective-permute-start.8 = (bf16[4,16,512]{2,1,0:T(8,128)(2,1)S(1)}, bf16[4,16,512]{2,1,0:T(8,128)(2,1)S(1)}, u32[]{:S(2)}, u32[]{:S(2)}) collective-permute-start(bf16[4,16,512]{2,1,0:T(8,128)(2,1)S(1)} %get-tuple-element.33.held_ref), channel_id=1, source_target_pairs={{0,4},{4,0},{8,12},{12,8},{16,20},{20,16},{24,28},{28,24},{1,5},{5... | collective-permute-start | bytes 196616 | tf_op jit(solution)/shard_map/ppermute | solution.py:139
  17.8 1.2 %collective-permute-start.6 = (f32[16,256]{1,0:T(8,128)S(1)}, f32[16,256]{1,0:T(8,128)S(1)}, u32[]{:S(2)}, u32[]{:S(2)}) collective-permute-start(f32[16,256]{1,0:T(8,128)S(1)} %low.1), channel_id=1, source_target_pairs={{0,1},{1,0},{2,3},{3,2},{4,5},{5,4},{6,7},{7,6},{8,9},{9,8},{10,11... | collective-permute-start | bytes 49160 | tf_op jit(solution)/shard_map/ppermute | solution.py:139
  19.0 3.2 %collective-permute-start.7 = (f32[16,256]{1,0:T(8,128)S(1)}, f32[16,256]{1,0:T(8,128)S(1)}, u32[]{:S(2)}, u32[]{:S(2)}) collective-permute-start(f32[16,256]{1,0:T(8,128)S(1)} %add.11.low0_ref), channel_id=1, source_target_pairs={{0,3},{1,2},{2,1},{3,0},{4,7},{5,6},{6,5},{7,4},{8,11},{9,10},{10,... | collective-permute-start | bytes 49160 | tf_op jit(solution)/shard_map/ppermute | solution.py:139

commit v4 on v3

--- a/solution.py
+++ b/solution.py
@@ -12,6 +12,7 @@
 VMEM = pl.BlockSpec(memory_space=pltpu.VMEM)
 HBM = pl.BlockSpec(memory_space=pltpu.HBM)
 F32, BF16 = jnp.float32, jnp.bfloat16
+CHUNKS = 2
 
 
 def dot(a, b, contract):
@@ -100,7 +101,7 @@
     part = far_ref.shape[1]
     mine = lax.axis_index("tp")
     copies[6].wait()
-    for k, ref in ((3, far_ref), (2, mid_ref), (1, near_ref), (0, own_ref)):
+    for k, ref in ((2, far_ref), (3, mid_ref), (1, near_ref), (0, own_ref)):
         block = w_ref[:, pl.ds(pl.multiple_of((mine ^ k) * part, part), part)]
         ref[...] = dot(att, block, (1, 0)).astype(ref.dtype)
 
@@ -122,28 +123,38 @@
     low_ref[...] = total
 
 
-def final_kernel(place_ref, own_ref, near_ref, far_ref, low0_ref, low1_ref, held_ref, came_ref, out_ref):
+def base_kernel(own_ref, near_ref, far_ref, base_ref):
+    base_ref[...] = own_ref[...] + near_ref[...].astype(F32) + far_ref[...].astype(F32)
+
+
+def final_kernel(place_ref, base_ref, low0_ref, low1_ref, low2_ref, low3_ref, held_ref, came_ref, out_hbm, out_ref, sems):
     rank, rows = low0_ref.shape
     blocks, _, part = held_ref.shape
-    low = low0_ref[...] + low1_ref[...]
+    low = (low0_ref[...] + low1_ref[...]) + (low2_ref[...] + low3_ref[...])
     spread = jnp.where(of_prompt(place_ref, rank, 2 * blocks), jnp.concatenate([low] * (2 * blocks), axis=0), 0.0)
     uppers = jnp.concatenate([ref[...].reshape(blocks * rank, part) for ref in (held_ref, came_ref)], axis=0)
     high = spread.astype(BF16)
     rest = (spread - high.astype(F32)).astype(BF16)
-    delta = dot(high, uppers, (0, 0)) + dot(rest, uppers, (0, 0))
-    base = own_ref[...] + near_ref[...].astype(F32) + far_ref[...].astype(F32)
-    out_ref[...] = (base + delta).astype(BF16)
+    copies = []
+    for c in range(CHUNKS):
+        mine = slice(c * rows // CHUNKS, (c + 1) * rows // CHUNKS)
+        delta = dot(high[:, mine], uppers, (0, 0)) + dot(rest[:, mine], uppers, (0, 0))
+        out_ref[mine, :] = (base_ref[mine, :] + delta).astype(BF16)
+        copies.append(pltpu.make_async_copy(out_ref.at[mine], out_hbm.at[mine], sems.at[c]))
+        copies[-1].start()
+    for copy in copies:
+        copy.wait()
 
 
 def swap(array, axis, size, k):
     return lax.ppermute(array, axis, [(i, i ^ k) for i in range(size)])
 
 
-def call(kernel, name, operands, specs, out, mib, us, scratch=(), place=pltpu.VMEM):
+def call(kernel, name, operands, specs, out, mib, us, scratch=(), place=pltpu.VMEM, out_spec=VMEM):
     return pl.pallas_call(
         kernel,
         in_specs=specs,
-        out_specs=[VMEM] * len(out),
+        out_specs=[out_spec] * len(out),
         out_shape=[place(s, d) for s, d in out],
         scratch_shapes=scratch,
         compiler_params=pltpu.CompilerParams(vmem_limit_bytes=mib << 20),
@@ -184,7 +195,7 @@
     from_near = swap(far_part, "tp", n_tp, 1)
     near = swap(near_part, "tp", n_tp, 1)
     to_far = (mid_part + from_near.astype(F32)).astype(BF16)
-    from_far = swap(to_far, "tp", n_tp, 2)
+    from_far = swap(to_far, "tp", n_tp, 3)
     for j, k in enumerate(hops[1:-1]):
         came = swap(held, "req", n_req, k)
         if j == 0:
@@ -195,16 +206,19 @@
     ups_came = swap(ups, "req", n_req, hops[-1])
 
     (low,) = call(low_kernel, "low", (place, att, downs, downs_came), [VMEM] * 4, [((rank, rows), F32)], 16, 0.3)
-    low = low + swap(low, "tp", n_tp, 1)
+    lows = [low] + [swap(low, "tp", n_tp, k) for k in (3, 2, 1)]
+    (base,) = call(base_kernel, "base", (own_part, near, from_far), [VMEM] * 3, [((rows, part), F32)], 8, 0.2)
     (out,) = call(
         final_kernel,
         "final",
-        (place, own_part, near, from_far, low, swap(low, "tp", n_tp, 3), ups, ups_came),
+        (place, base, *lows, ups, ups_came),
         [VMEM] * 8,
         [((rows, part), BF16)],
         24,
         1,
-        place=jax.ShapeDtypeStruct,
+        [pltpu.VMEM((rows, part), BF16), pltpu.SemaphoreType.DMA((CHUNKS,))],
+        jax.ShapeDtypeStruct,
+        HBM,
     )
     return out
 

time: 23.5 us -> 22.9 us (0.974)
  waiting for transfers between devices: 6.38 us -> 5.77 us
    ppermute x9 -> x10, waiting for transfers between devices: 6.38 us -> 5.77 us  [swap(): return lax.ppermute(array, axis, [(i, i ^ k) for i in range(size)])]
    pallas_call x3 -> x4, Pallas kernels: 3.95 us -> 3.99 us  [call(): pl.pallas_call(kernel, in_specs=specs, out_specs=[out_spec] * len(out), o...]
    ppermute x9 -> x10, starting transfers between devices: 11.2 us -> 11.2 us  [swap(): return lax.ppermute(array, axis, [(i, i ^ k) for i in range(size)])]
  transfers between devices with their start and end apart: 9 -> 10, of which waited for: 4 -> 4; matrix products, arithmetic and copies ran while one was open for 0% -> 0% of each run, Pallas kernels for 13% -> 13%
where the time goes in v4:
time: 22.9 us; the launch traced here: 22.7 us
  starting transfers between devices  11.2 us (49%)
  waiting for transfers between devices  5.77 us (25%)
  Pallas kernels  3.99 us (17%)
  local copies, waits for them, and re-layouts  0.87 us (4%)
  other arithmetic  0.8 us (3%)
    ppermute x10, starting transfers between devices, swap(): return lax.ppermute(array, axis, [(i, i ^ k) for i in range(size)])  11.2 us
    ppermute x10, waiting for transfers between devices, swap(): return lax.ppermute(array, axis, [(i, i ^ k) for i in range(size)])  5.77 us
    pallas_call x4, Pallas kernels, call(): pl.pallas_call(kernel, in_specs=specs, out_specs=[out_spec] * len(out), o...  3.99 us
    unnamed x4, local copies, waits for them, and re-layouts  0.85 us
    broadcast_in_dim x1, other arithmetic, body(): held = jnp.concatenate([adapter_down[0].T, own_up], axis=0)[None]  0.72 us
  transfers between devices with their start and end apart: 10, of which 4 were waited for; matrix products, arithmetic and copies ran while one was open for 0% of the time, Pallas kernels for 13%

profile of v4, /device:TPU:0, one launch (start us, length us, event | category | flops | bytes accessed | tf_op | source)
XLA Modules:
  0.0 22.7 jit_solution(16680817584328367789)
XLA Ops:
  0.0 0.8 %copy-done = bf16[1,16,2048]{2,1,0:T(8,128)(2,1)S(1)} copy-done((bf16[1,16,2048]{2,1,0:T(8,128)(2,1)S(1)}, bf16[1,16,2048]{2,1,0:T(8,128)(2,1)}, u32[]{:S(2)}) %copy-start) | copy-done | bytes 65560
  0.8 0.7 %maximum_bitcast_fusion = bf16[1,32,512]{2,1,0:T(8,128)(2,1)S(1)} fusion(bf16[16,512]{1,0:T(8,128)(2,1)S(1)} %dynamic-slice_bitcast_fusion, bf16[16,512]{1,0:T(8,128)(2,1)} %bitcast.7), kind=kLoop, calls=%fused_computation.1 | loop fusion | flops 65536 | bytes 65536 | tf_op jit(solution)/shard_map/broadcast_in_dim | solution.py:174
  1.6 4.0 %collective-permute-start = (bf16[1,32,512]{2,1,0:T(8,128)(2,1)S(1)}, bf16[1,32,512]{2,1,0:T(8,128)(2,1)S(1)}, u32[]{:S(2)}, u32[]{:S(2)}) collective-permute-start(bf16[1,32,512]{2,1,0:T(8,128)(2,1)S(1)} %maximum_bitcast_fusion), channel_id=1, source_target_pairs={{0,16},{4,20},{8,24},{12,28},{16,0},{20,4},{24,8},{28,12},{1,17},{... | collective-permute-start | bytes 98312 | tf_op jit(solution)/shard_map/ppermute | solution.py:150
  5.6 2.6 %attend.1 = (bf16[256,512]{1,0:T(8,128)(2,1)S(1)}, s32[8,256]{1,0:T(8,128)S(1)}, bf16[256,512]{1,0:T(8,128)(2,1)S(1)}, bf16[256,512]{1,0:T(8,128)(2,1)S(1)}, f32...) custom-call(bf16[256,512]{1,0:T(8,128)(2,1)} %q_hbm, bf16[256,512]{1,0:T(8,128)(2,1)} %k_hbm.1, bf16[256,512]{1,0:T(8,128)(2,1)} %v_hbm.1, ...), custom_call_target="tpu_custom_call" | custom-call | flops 3000000000 | bytes 10800000 | tf_op jit(solution)/shard_map/attend/pallas_call | solution.py:154
  8.3 0.1 collective-permute-start.2
  8.3 0.5 %collective-permute-start.1 = (bf16[256,512]{1,0:T(8,128)(2,1)S(1)}, bf16[256,512]{1,0:T(8,128)(2,1)S(1)}, u32[]{:S(2)}, u32[]{:S(2)}) collective-permute-start(bf16[256,512]{1,0:T(8,128)(2,1)S(1)} %get-tuple-element.25), channel_id=1, source_target_pairs={{0,1},{1,0},{2,3},{3,2},{4,5},{5,4},{6,7},{7,6},{8,9},{9,8},{10,11... | collective-permute-start | bytes 786440 | tf_op jit(solution)/shard_map/ppermute | solution.py:150
  8.8 1.6 %collective-permute-start.4 = (bf16[2,32,512]{2,1,0:T(8,128)(2,1)S(1)}, bf16[2,32,512]{2,1,0:T(8,128)(2,1)S(1)}, u32[]{:S(2)}, u32[]{:S(2)}) collective-permute-start(bf16[2,32,512]{2,1,0:T(8,128)(2,1)S(1)} %constant_dynamic-update-slice_fusion), channel_id=1, source_target_pairs={{0,8},{4,12},{8,0},{12,4},{16,24},{20,28},{24,16},{28,20},{1,9},{5... | collective-permute-start | bytes 196616 | tf_op jit(solution)/shard_map/ppermute | solution.py:150
  10.4 0.0 collective-permute-done.2
  10.4 0.1 add_convert_fusion
  10.5 1.0 %collective-permute-start.3 = (bf16[256,512]{1,0:T(8,128)(2,1)S(1)}, bf16[256,512]{1,0:T(8,128)(2,1)S(1)}, u32[]{:S(2)}, u32[]{:S(2)}) collective-permute-start(bf16[256,512]{1,0:T(8,128)(2,1)S(1)} %add_convert_fusion), channel_id=1, source_target_pairs={{0,3},{1,2},{2,1},{3,0},{4,7},{5,6},{6,5},{7,4},{8,11},{9,10},{10,... | collective-permute-start | bytes 786440 | tf_op jit(solution)/shard_map/ppermute | solution.py:150
  11.5 1.6 %collective-permute-done.4 = bf16[2,32,512]{2,1,0:T(8,128)(2,1)S(1)} collective-permute-done((bf16[2,32,512]{2,1,0:T(8,128)(2,1)S(1)}, bf16[2,32,512]{2,1,0:T(8,128)(2,1)S(1)}, u32[]{:S(2)}, u32[]{:S(2)}) %collective-permute-start.4) | collective-permute-done | bytes 65568 | tf_op jit(solution)/shard_map/ppermute | solution.py:150
  13.1 1.6 %collective-permute-start.5 = (bf16[4,16,512]{2,1,0:T(8,128)(2,1)S(1)}, bf16[4,16,512]{2,1,0:T(8,128)(2,1)S(1)}, u32[]{:S(2)}, u32[]{:S(2)}) collective-permute-start(bf16[4,16,512]{2,1,0:T(8,128)(2,1)S(1)} %get-tuple-element.34.held_ref), channel_id=1, source_target_pairs={{0,4},{4,0},{8,12},{12,8},{16,20},{20,16},{24,28},{28,24},{1,5},{5... | collective-permute-start | bytes 196616 | tf_op jit(solution)/shard_map/ppermute | solution.py:150
  14.7 0.5 %collective-permute-start.9 = (bf16[4,16,512]{2,1,0:T(8,128)(2,1)S(1)}, bf16[4,16,512]{2,1,0:T(8,128)(2,1)S(1)}, u32[]{:S(2)}, u32[]{:S(2)}) collective-permute-start(bf16[4,16,512]{2,1,0:T(8,128)(2,1)S(1)} %get-tuple-element.33.held_ref), channel_id=1, source_target_pairs={{0,4},{4,0},{8,12},{12,8},{16,20},{20,16},{24,28},{28,24},{1,5},{5... | collective-permute-start | bytes 196616 | tf_op jit(solution)/shard_map/ppermute | solution.py:150
  15.2 2.3 %collective-permute-done.5.came_ref = bf16[4,16,512]{2,1,0:T(8,128)(2,1)S(1)} collective-permute-done((bf16[4,16,512]{2,1,0:T(8,128)(2,1)S(1)}, bf16[4,16,512]{2,1,0:T(8,128)(2,1)S(1)}, u32[]{:S(2)}, u32[]{:S(2)}) %collective-permute-start.5) | collective-permute-done | bytes 65568 | tf_op jit(solution)/shard_map/ppermute | solution.py:150
  17.5 0.3 %low.1.low0_ref = f32[16,256]{1,0:T(8,128)S(1)} custom-call(s32[8,256]{1,0:T(8,128)S(1)} %get-tuple-element.20.place_ref, bf16[256,512]{1,0:T(8,128)(2,1)S(1)} %get-tuple-element.28.att_ref, bf16[4,16,512]{2,1,0:T(8,128)(2,1)S(1)} %get-tuple-element.34.held_ref, bf16[4,16,512]{2,1,0:T(8,128)(2,1)S(1)} %collective-permute-done.5.came_ref), custom_call_target="tpu_custom_call" | custom-call | flops 300000000 | bytes 1080000 | tf_op jit(solution)/shard_map/low/pallas_call | solution.py:154
  17.8 0.1 collective-permute-start.6
  17.9 1.5 %collective-permute-start.7 = (f32[16,256]{1,0:T(8,128)S(1)}, f32[16,256]{1,0:T(8,128)S(1)}, u32[]{:S(2)}, u32[]{:S(2)}) collective-permute-start(f32[16,256]{1,0:T(8,128)S(1)} %low.1.low0_ref), channel_id=1, source_target_pairs={{0,2},{1,3},{2,0},{3,1},{4,6},{5,7},{6,4},{7,5},{8,10},{9,11},{10,... | collective-permute-start | bytes 49160 | tf_op jit(solution)/shard_map/ppermute | solution.py:150
  19.4 0.0 collective-permute-done.1.near_ref
  19.4 0.3 %collective-permute-start.8 = (f32[16,256]{1,0:T(8,128)S(1)}, f32[16,256]{1,0:T(8,128)S(1)}, u32[]{:S(2)}, u32[]{:S(2)}) collective-permute-start(f32[16,256]{1,0:T(8,128)S(1)} %low.1.low0_ref), channel_id=1, source_target_pairs={{0,1},{1,0},{2,3},{3,2},{4,5},{5,4},{6,7},{7,6},{8,9},{9,8},{10,11... | collective-permute-start | bytes 49160 | tf_op jit(solution)/shard_map/ppermute | solution.py:150
  19.7 0.0 collective-permute-done.3.far_ref
  19.7 0.1 base.1.base_ref
  19.8 1.4 %collective-permute-done.6.low1_ref = f32[16,256]{1,0:T(8,128)S(1)} collective-permute-done((f32[16,256]{1,0:T(8,128)S(1)}, f32[16,256]{1,0:T(8,128)S(1)}, u32[]{:S(2)}, u32[]{:S(2)}) %collective-permute-start.6) | collective-permute-done | bytes 16416 | tf_op jit(solution)/shard_map/ppermute | solution.py:150
  21.2 0.5 %collective-permute-done.7.low2_ref = f32[16,256]{1,0:T(8,128)S(1)} collective-permute-done((f32[16,256]{1,0:T(8,128)S(1)}, f32[16,256]{1,0:T(8,128)S(1)}, u32[]{:S(2)}, u32[]{:S(2)}) %collective-permute-start.7) | collective-permute-done | bytes 16416 | tf_op jit(solution)/shard_map/ppermute | solution.py:150
  21.7 1.0 %final.1 = bf16[256,512]{1,0:T(8,128)(2,1)} custom-call(s32[8,256]{1,0:T(8,128)S(1)} %get-tuple-element.20.place_ref, f32[256,512]{1,0:T(8,128)S(1)} %base.1.base_ref, f32[16,256]{1,0:T(8,128)S(1)} %low.1.low0_ref, f32[16,256]{1,0:T(8,128)S(1)} %collective-permute-done.6.low1_ref, f32[16,256]{1,0:T(8,128)S(1)} %collective-permute-done.7.low2_ref, ...), custom_call_target="tpu_custom_call" | custom-call | flops 1000000000 | bytes 3600000 | tf_op jit(solution)/shard_map/final/pallas_call | solution.py:154
  (10 shorter events, 0.0 us)
Async XLA Ops:
  0.0 0.8 %copy-start = (bf16[1,16,2048]{2,1,0:T(8,128)(2,1)S(1)}, bf16[1,16,2048]{2,1,0:T(8,128)(2,1)}, u32[]{:S(2)}) copy-start(bf16[1,16,2048]{2,1,0:T(8,128)(2,1)} %param.16) | copy-start | bytes 196612
  1.6 6.7 %collective-permute-start = (bf16[1,32,512]{2,1,0:T(8,128)(2,1)S(1)}, bf16[1,32,512]{2,1,0:T(8,128)(2,1)S(1)}, u32[]{:S(2)}, u32[]{:S(2)}) collective-permute-start(bf16[1,32,512]{2,1,0:T(8,128)(2,1)S(1)} %maximum_bitcast_fusion), channel_id=1, source_target_pairs={{0,16},{4,20},{8,24},{12,28},{16,0},{20,4},{24,8},{28,12},{1,17},{... | collective-permute-start | bytes 98312 | tf_op jit(solution)/shard_map/ppermute | solution.py:150
  8.3 2.2 %collective-permute-start.2 = (bf16[256,512]{1,0:T(8,128)(2,1)S(1)}, bf16[256,512]{1,0:T(8,128)(2,1)S(1)}, u32[]{:S(2)}, u32[]{:S(2)}) collective-permute-start(bf16[256,512]{1,0:T(8,128)(2,1)S(1)} %get-tuple-element.27), channel_id=1, source_target_pairs={{0,1},{1,0},{2,3},{3,2},{4,5},{5,4},{6,7},{7,6},{8,9},{9,8},{10,11... | collective-permute-start | bytes 786440 | tf_op jit(solution)/shard_map/ppermute | solution.py:150
  8.3 11.1 %collective-permute-start.1 = (bf16[256,512]{1,0:T(8,128)(2,1)S(1)}, bf16[256,512]{1,0:T(8,128)(2,1)S(1)}, u32[]{:S(2)}, u32[]{:S(2)}) collective-permute-start(bf16[256,512]{1,0:T(8,128)(2,1)S(1)} %get-tuple-element.25), channel_id=1, source_target_pairs={{0,1},{1,0},{2,3},{3,2},{4,5},{5,4},{6,7},{7,6},{8,9},{9,8},{10,11... | collective-permute-start | bytes 786440 | tf_op jit(solution)/shard_map/ppermute | solution.py:150
  8.8 4.3 %collective-permute-start.4 = (bf16[2,32,512]{2,1,0:T(8,128)(2,1)S(1)}, bf16[2,32,512]{2,1,0:T(8,128)(2,1)S(1)}, u32[]{:S(2)}, u32[]{:S(2)}) collective-permute-start(bf16[2,32,512]{2,1,0:T(8,128)(2,1)S(1)} %constant_dynamic-update-slice_fusion), channel_id=1, source_target_pairs={{0,8},{4,12},{8,0},{12,4},{16,24},{20,28},{24,16},{28,20},{1,9},{5... | collective-permute-start | bytes 196616 | tf_op jit(solution)/shard_map/ppermute | solution.py:150
  10.5 9.2 %collective-permute-start.3 = (bf16[256,512]{1,0:T(8,128)(2,1)S(1)}, bf16[256,512]{1,0:T(8,128)(2,1)S(1)}, u32[]{:S(2)}, u32[]{:S(2)}) collective-permute-start(bf16[256,512]{1,0:T(8,128)(2,1)S(1)} %add_convert_fusion), channel_id=1, source_target_pairs={{0,3},{1,2},{2,1},{3,0},{4,7},{5,6},{6,5},{7,4},{8,11},{9,10},{10,... | collective-permute-start | bytes 786440 | tf_op jit(solution)/shard_map/ppermute | solution.py:150
  13.1 4.4 %collective-permute-start.5 = (bf16[4,16,512]{2,1,0:T(8,128)(2,1)S(1)}, bf16[4,16,512]{2,1,0:T(8,128)(2,1)S(1)}, u32[]{:S(2)}, u32[]{:S(2)}) collective-permute-start(bf16[4,16,512]{2,1,0:T(8,128)(2,1)S(1)} %get-tuple-element.34.held_ref), channel_id=1, source_target_pairs={{0,4},{4,0},{8,12},{12,8},{16,20},{20,16},{24,28},{28,24},{1,5},{5... | collective-permute-start | bytes 196616 | tf_op jit(solution)/shard_map/ppermute | solution.py:150
  14.7 5.1 %collective-permute-start.9 = (bf16[4,16,512]{2,1,0:T(8,128)(2,1)S(1)}, bf16[4,16,512]{2,1,0:T(8,128)(2,1)S(1)}, u32[]{:S(2)}, u32[]{:S(2)}) collective-permute-start(bf16[4,16,512]{2,1,0:T(8,128)(2,1)S(1)} %get-tuple-element.33.held_ref), channel_id=1, source_target_pairs={{0,4},{4,0},{8,12},{12,8},{16,20},{20,16},{24,28},{28,24},{1,5},{5... | collective-permute-start | bytes 196616 | tf_op jit(solution)/shard_map/ppermute | solution.py:150
  17.8 3.4 %collective-permute-start.6 = (f32[16,256]{1,0:T(8,128)S(1)}, f32[16,256]{1,0:T(8,128)S(1)}, u32[]{:S(2)}, u32[]{:S(2)}) collective-permute-start(f32[16,256]{1,0:T(8,128)S(1)} %low.1.low0_ref), channel_id=1, source_target_pairs={{0,3},{1,2},{2,1},{3,0},{4,7},{5,6},{6,5},{7,4},{8,11},{9,10},{10,... | collective-permute-start | bytes 49160 | tf_op jit(solution)/shard_map/ppermute | solution.py:150
  17.9 3.8 %collective-permute-start.7 = (f32[16,256]{1,0:T(8,128)S(1)}, f32[16,256]{1,0:T(8,128)S(1)}, u32[]{:S(2)}, u32[]{:S(2)}) collective-permute-start(f32[16,256]{1,0:T(8,128)S(1)} %low.1.low0_ref), channel_id=1, source_target_pairs={{0,2},{1,3},{2,0},{3,1},{4,6},{5,7},{6,4},{7,5},{8,10},{9,11},{10,... | collective-permute-start | bytes 49160 | tf_op jit(solution)/shard_map/ppermute | solution.py:150
  19.4 2.3 %collective-permute-start.8 = (f32[16,256]{1,0:T(8,128)S(1)}, f32[16,256]{1,0:T(8,128)S(1)}, u32[]{:S(2)}, u32[]{:S(2)}) collective-permute-start(f32[16,256]{1,0:T(8,128)S(1)} %low.1.low0_ref), channel_id=1, source_target_pairs={{0,1},{1,0},{2,3},{3,2},{4,5},{5,4},{6,7},{7,6},{8,9},{9,8},{10,11... | collective-permute-start | bytes 49160 | tf_op jit(solution)/shard_map/ppermute | solution.py:150

commit v5 on v4

--- a/solution.py
+++ b/solution.py
@@ -135,10 +135,12 @@
     uppers = jnp.concatenate([ref[...].reshape(blocks * rank, part) for ref in (held_ref, came_ref)], axis=0)
     high = spread.astype(BF16)
     rest = (spread - high.astype(F32)).astype(BF16)
+    spread = jnp.concatenate([high, rest], axis=0).T
+    uppers = jnp.concatenate([uppers, uppers], axis=0)
     copies = []
     for c in range(CHUNKS):
         mine = slice(c * rows // CHUNKS, (c + 1) * rows // CHUNKS)
-        delta = dot(high[:, mine], uppers, (0, 0)) + dot(rest[:, mine], uppers, (0, 0))
+        delta = dot(spread[mine], uppers, (1, 0))
         out_ref[mine, :] = (base_ref[mine, :] + delta).astype(BF16)
         copies.append(pltpu.make_async_copy(out_ref.at[mine], out_hbm.at[mine], sems.at[c]))
         copies[-1].start()

time: 22.9 us -> 22.9 us (level)
  no operation moved by 1% of the time
where the time goes in v5:
time: 22.9 us; the launch traced here: 22.6 us
  starting transfers between devices  11.2 us (49%)
  waiting for transfers between devices  5.77 us (25%)
  Pallas kernels  3.93 us (17%)
  local copies, waits for them, and re-layouts  0.87 us (4%)
  other arithmetic  0.8 us (3%)
    ppermute x10, starting transfers between devices, swap(): return lax.ppermute(array, axis, [(i, i ^ k) for i in range(size)])  11.2 us
    ppermute x10, waiting for transfers between devices, swap(): return lax.ppermute(array, axis, [(i, i ^ k) for i in range(size)])  5.77 us
    pallas_call x4, Pallas kernels, call(): pl.pallas_call(kernel, in_specs=specs, out_specs=[out_spec] * len(out), o...  3.93 us
    unnamed x4, local copies, waits for them, and re-layouts  0.85 us
    broadcast_in_dim x1, other arithmetic, body(): held = jnp.concatenate([adapter_down[0].T, own_up], axis=0)[None]  0.72 us
  transfers between devices with their start and end apart: 10, of which 4 were waited for; matrix products, arithmetic and copies ran while one was open for 0% of the time, Pallas kernels for 13%

profile of v5, /device:TPU:0, one launch (start us, length us, event | category | flops | bytes accessed | tf_op | source)
XLA Modules:
  0.0 22.6 jit_solution(6254196606339051694)
XLA Ops:
  0.0 0.8 %copy-done = bf16[1,16,2048]{2,1,0:T(8,128)(2,1)S(1)} copy-done((bf16[1,16,2048]{2,1,0:T(8,128)(2,1)S(1)}, bf16[1,16,2048]{2,1,0:T(8,128)(2,1)}, u32[]{:S(2)}) %copy-start) | copy-done | bytes 65560
  0.8 0.7 %maximum_bitcast_fusion = bf16[1,32,512]{2,1,0:T(8,128)(2,1)S(1)} fusion(bf16[16,512]{1,0:T(8,128)(2,1)S(1)} %dynamic-slice_bitcast_fusion, bf16[16,512]{1,0:T(8,128)(2,1)} %bitcast.7), kind=kLoop, calls=%fused_computation.1 | loop fusion | flops 65536 | bytes 65536 | tf_op jit(solution)/shard_map/broadcast_in_dim | solution.py:176
  1.6 4.0 %collective-permute-start = (bf16[1,32,512]{2,1,0:T(8,128)(2,1)S(1)}, bf16[1,32,512]{2,1,0:T(8,128)(2,1)S(1)}, u32[]{:S(2)}, u32[]{:S(2)}) collective-permute-start(bf16[1,32,512]{2,1,0:T(8,128)(2,1)S(1)} %maximum_bitcast_fusion), channel_id=1, source_target_pairs={{0,16},{4,20},{8,24},{12,28},{16,0},{20,4},{24,8},{28,12},{1,17},{... | collective-permute-start | bytes 98312 | tf_op jit(solution)/shard_map/ppermute | solution.py:152
  5.6 2.6 %attend.1 = (bf16[256,512]{1,0:T(8,128)(2,1)S(1)}, s32[8,256]{1,0:T(8,128)S(1)}, bf16[256,512]{1,0:T(8,128)(2,1)S(1)}, bf16[256,512]{1,0:T(8,128)(2,1)S(1)}, f32...) custom-call(bf16[256,512]{1,0:T(8,128)(2,1)} %q_hbm, bf16[256,512]{1,0:T(8,128)(2,1)} %k_hbm.1, bf16[256,512]{1,0:T(8,128)(2,1)} %v_hbm.1, ...), custom_call_target="tpu_custom_call" | custom-call | flops 3000000000 | bytes 10800000 | tf_op jit(solution)/shard_map/attend/pallas_call | solution.py:156
  8.3 0.1 collective-permute-start.2
  8.3 0.5 %collective-permute-start.1 = (bf16[256,512]{1,0:T(8,128)(2,1)S(1)}, bf16[256,512]{1,0:T(8,128)(2,1)S(1)}, u32[]{:S(2)}, u32[]{:S(2)}) collective-permute-start(bf16[256,512]{1,0:T(8,128)(2,1)S(1)} %get-tuple-element.25), channel_id=1, source_target_pairs={{0,1},{1,0},{2,3},{3,2},{4,5},{5,4},{6,7},{7,6},{8,9},{9,8},{10,11... | collective-permute-start | bytes 786440 | tf_op jit(solution)/shard_map/ppermute | solution.py:152
  8.8 1.6 %collective-permute-start.4 = (bf16[2,32,512]{2,1,0:T(8,128)(2,1)S(1)}, bf16[2,32,512]{2,1,0:T(8,128)(2,1)S(1)}, u32[]{:S(2)}, u32[]{:S(2)}) collective-permute-start(bf16[2,32,512]{2,1,0:T(8,128)(2,1)S(1)} %constant_dynamic-update-slice_fusion), channel_id=1, source_target_pairs={{0,8},{4,12},{8,0},{12,4},{16,24},{20,28},{24,16},{28,20},{1,9},{5... | collective-permute-start | bytes 196616 | tf_op jit(solution)/shard_map/ppermute | solution.py:152
  10.4 0.0 collective-permute-done.2
  10.4 0.1 add_convert_fusion
  10.5 1.0 %collective-permute-start.3 = (bf16[256,512]{1,0:T(8,128)(2,1)S(1)}, bf16[256,512]{1,0:T(8,128)(2,1)S(1)}, u32[]{:S(2)}, u32[]{:S(2)}) collective-permute-start(bf16[256,512]{1,0:T(8,128)(2,1)S(1)} %add_convert_fusion), channel_id=1, source_target_pairs={{0,3},{1,2},{2,1},{3,0},{4,7},{5,6},{6,5},{7,4},{8,11},{9,10},{10,... | collective-permute-start | bytes 786440 | tf_op jit(solution)/shard_map/ppermute | solution.py:152
  11.5 1.6 %collective-permute-done.4 = bf16[2,32,512]{2,1,0:T(8,128)(2,1)S(1)} collective-permute-done((bf16[2,32,512]{2,1,0:T(8,128)(2,1)S(1)}, bf16[2,32,512]{2,1,0:T(8,128)(2,1)S(1)}, u32[]{:S(2)}, u32[]{:S(2)}) %collective-permute-start.4) | collective-permute-done | bytes 65568 | tf_op jit(solution)/shard_map/ppermute | solution.py:152
  13.1 1.6 %collective-permute-start.5 = (bf16[4,16,512]{2,1,0:T(8,128)(2,1)S(1)}, bf16[4,16,512]{2,1,0:T(8,128)(2,1)S(1)}, u32[]{:S(2)}, u32[]{:S(2)}) collective-permute-start(bf16[4,16,512]{2,1,0:T(8,128)(2,1)S(1)} %get-tuple-element.34.held_ref), channel_id=1, source_target_pairs={{0,4},{4,0},{8,12},{12,8},{16,20},{20,16},{24,28},{28,24},{1,5},{5... | collective-permute-start | bytes 196616 | tf_op jit(solution)/shard_map/ppermute | solution.py:152
  14.7 0.5 %collective-permute-start.9 = (bf16[4,16,512]{2,1,0:T(8,128)(2,1)S(1)}, bf16[4,16,512]{2,1,0:T(8,128)(2,1)S(1)}, u32[]{:S(2)}, u32[]{:S(2)}) collective-permute-start(bf16[4,16,512]{2,1,0:T(8,128)(2,1)S(1)} %get-tuple-element.33.held_ref), channel_id=1, source_target_pairs={{0,4},{4,0},{8,12},{12,8},{16,20},{20,16},{24,28},{28,24},{1,5},{5... | collective-permute-start | bytes 196616 | tf_op jit(solution)/shard_map/ppermute | solution.py:152
  15.2 2.3 %collective-permute-done.5.came_ref = bf16[4,16,512]{2,1,0:T(8,128)(2,1)S(1)} collective-permute-done((bf16[4,16,512]{2,1,0:T(8,128)(2,1)S(1)}, bf16[4,16,512]{2,1,0:T(8,128)(2,1)S(1)}, u32[]{:S(2)}, u32[]{:S(2)}) %collective-permute-start.5) | collective-permute-done | bytes 65568 | tf_op jit(solution)/shard_map/ppermute | solution.py:152
  17.5 0.3 %low.1.low0_ref = f32[16,256]{1,0:T(8,128)S(1)} custom-call(s32[8,256]{1,0:T(8,128)S(1)} %get-tuple-element.20.place_ref, bf16[256,512]{1,0:T(8,128)(2,1)S(1)} %get-tuple-element.28.att_ref, bf16[4,16,512]{2,1,0:T(8,128)(2,1)S(1)} %get-tuple-element.34.held_ref, bf16[4,16,512]{2,1,0:T(8,128)(2,1)S(1)} %collective-permute-done.5.came_ref), custom_call_target="tpu_custom_call" | custom-call | flops 300000000 | bytes 1080000 | tf_op jit(solution)/shard_map/low/pallas_call | solution.py:156
  17.8 0.1 collective-permute-start.6
  17.9 1.5 %collective-permute-start.7 = (f32[16,256]{1,0:T(8,128)S(1)}, f32[16,256]{1,0:T(8,128)S(1)}, u32[]{:S(2)}, u32[]{:S(2)}) collective-permute-start(f32[16,256]{1,0:T(8,128)S(1)} %low.1.low0_ref), channel_id=1, source_target_pairs={{0,2},{1,3},{2,0},{3,1},{4,6},{5,7},{6,4},{7,5},{8,10},{9,11},{10,... | collective-permute-start | bytes 49160 | tf_op jit(solution)/shard_map/ppermute | solution.py:152
  19.4 0.0 collective-permute-done.1.near_ref
  19.4 0.3 %collective-permute-start.8 = (f32[16,256]{1,0:T(8,128)S(1)}, f32[16,256]{1,0:T(8,128)S(1)}, u32[]{:S(2)}, u32[]{:S(2)}) collective-permute-start(f32[16,256]{1,0:T(8,128)S(1)} %low.1.low0_ref), channel_id=1, source_target_pairs={{0,1},{1,0},{2,3},{3,2},{4,5},{5,4},{6,7},{7,6},{8,9},{9,8},{10,11... | collective-permute-start | bytes 49160 | tf_op jit(solution)/shard_map/ppermute | solution.py:152
  19.7 0.0 collective-permute-done.3.far_ref
  19.7 0.1 base.1.base_ref
  19.8 1.4 %collective-permute-done.6.low1_ref = f32[16,256]{1,0:T(8,128)S(1)} collective-permute-done((f32[16,256]{1,0:T(8,128)S(1)}, f32[16,256]{1,0:T(8,128)S(1)}, u32[]{:S(2)}, u32[]{:S(2)}) %collective-permute-start.6) | collective-permute-done | bytes 16416 | tf_op jit(solution)/shard_map/ppermute | solution.py:152
  21.2 0.5 %collective-permute-done.7.low2_ref = f32[16,256]{1,0:T(8,128)S(1)} collective-permute-done((f32[16,256]{1,0:T(8,128)S(1)}, f32[16,256]{1,0:T(8,128)S(1)}, u32[]{:S(2)}, u32[]{:S(2)}) %collective-permute-start.7) | collective-permute-done | bytes 16416 | tf_op jit(solution)/shard_map/ppermute | solution.py:152
  21.7 0.9 %final.1 = bf16[256,512]{1,0:T(8,128)(2,1)} custom-call(s32[8,256]{1,0:T(8,128)S(1)} %get-tuple-element.20.place_ref, f32[256,512]{1,0:T(8,128)S(1)} %base.1.base_ref, f32[16,256]{1,0:T(8,128)S(1)} %low.1.low0_ref, f32[16,256]{1,0:T(8,128)S(1)} %collective-permute-done.6.low1_ref, f32[16,256]{1,0:T(8,128)S(1)} %collective-permute-done.7.low2_ref, ...), custom_call_target="tpu_custom_call" | custom-call | flops 1000000000 | bytes 3600000 | tf_op jit(solution)/shard_map/final/pallas_call | solution.py:156
  (10 shorter events, 0.0 us)
Async XLA Ops:
  0.0 0.8 %copy-start = (bf16[1,16,2048]{2,1,0:T(8,128)(2,1)S(1)}, bf16[1,16,2048]{2,1,0:T(8,128)(2,1)}, u32[]{:S(2)}) copy-start(bf16[1,16,2048]{2,1,0:T(8,128)(2,1)} %param.16) | copy-start | bytes 196612
  1.6 6.7 %collective-permute-start = (bf16[1,32,512]{2,1,0:T(8,128)(2,1)S(1)}, bf16[1,32,512]{2,1,0:T(8,128)(2,1)S(1)}, u32[]{:S(2)}, u32[]{:S(2)}) collective-permute-start(bf16[1,32,512]{2,1,0:T(8,128)(2,1)S(1)} %maximum_bitcast_fusion), channel_id=1, source_target_pairs={{0,16},{4,20},{8,24},{12,28},{16,0},{20,4},{24,8},{28,12},{1,17},{... | collective-permute-start | bytes 98312 | tf_op jit(solution)/shard_map/ppermute | solution.py:152
  8.3 2.2 %collective-permute-start.2 = (bf16[256,512]{1,0:T(8,128)(2,1)S(1)}, bf16[256,512]{1,0:T(8,128)(2,1)S(1)}, u32[]{:S(2)}, u32[]{:S(2)}) collective-permute-start(bf16[256,512]{1,0:T(8,128)(2,1)S(1)} %get-tuple-element.27), channel_id=1, source_target_pairs={{0,1},{1,0},{2,3},{3,2},{4,5},{5,4},{6,7},{7,6},{8,9},{9,8},{10,11... | collective-permute-start | bytes 786440 | tf_op jit(solution)/shard_map/ppermute | solution.py:152
  8.3 11.1 %collective-permute-start.1 = (bf16[256,512]{1,0:T(8,128)(2,1)S(1)}, bf16[256,512]{1,0:T(8,128)(2,1)S(1)}, u32[]{:S(2)}, u32[]{:S(2)}) collective-permute-start(bf16[256,512]{1,0:T(8,128)(2,1)S(1)} %get-tuple-element.25), channel_id=1, source_target_pairs={{0,1},{1,0},{2,3},{3,2},{4,5},{5,4},{6,7},{7,6},{8,9},{9,8},{10,11... | collective-permute-start | bytes 786440 | tf_op jit(solution)/shard_map/ppermute | solution.py:152
  8.8 4.3 %collective-permute-start.4 = (bf16[2,32,512]{2,1,0:T(8,128)(2,1)S(1)}, bf16[2,32,512]{2,1,0:T(8,128)(2,1)S(1)}, u32[]{:S(2)}, u32[]{:S(2)}) collective-permute-start(bf16[2,32,512]{2,1,0:T(8,128)(2,1)S(1)} %constant_dynamic-update-slice_fusion), channel_id=1, source_target_pairs={{0,8},{4,12},{8,0},{12,4},{16,24},{20,28},{24,16},{28,20},{1,9},{5... | collective-permute-start | bytes 196616 | tf_op jit(solution)/shard_map/ppermute | solution.py:152
  10.5 9.2 %collective-permute-start.3 = (bf16[256,512]{1,0:T(8,128)(2,1)S(1)}, bf16[256,512]{1,0:T(8,128)(2,1)S(1)}, u32[]{:S(2)}, u32[]{:S(2)}) collective-permute-start(bf16[256,512]{1,0:T(8,128)(2,1)S(1)} %add_convert_fusion), channel_id=1, source_target_pairs={{0,3},{1,2},{2,1},{3,0},{4,7},{5,6},{6,5},{7,4},{8,11},{9,10},{10,... | collective-permute-start | bytes 786440 | tf_op jit(solution)/shard_map/ppermute | solution.py:152
  13.1 4.4 %collective-permute-start.5 = (bf16[4,16,512]{2,1,0:T(8,128)(2,1)S(1)}, bf16[4,16,512]{2,1,0:T(8,128)(2,1)S(1)}, u32[]{:S(2)}, u32[]{:S(2)}) collective-permute-start(bf16[4,16,512]{2,1,0:T(8,128)(2,1)S(1)} %get-tuple-element.34.held_ref), channel_id=1, source_target_pairs={{0,4},{4,0},{8,12},{12,8},{16,20},{20,16},{24,28},{28,24},{1,5},{5... | collective-permute-start | bytes 196616 | tf_op jit(solution)/shard_map/ppermute | solution.py:152
  14.7 5.1 %collective-permute-start.9 = (bf16[4,16,512]{2,1,0:T(8,128)(2,1)S(1)}, bf16[4,16,512]{2,1,0:T(8,128)(2,1)S(1)}, u32[]{:S(2)}, u32[]{:S(2)}) collective-permute-start(bf16[4,16,512]{2,1,0:T(8,128)(2,1)S(1)} %get-tuple-element.33.held_ref), channel_id=1, source_target_pairs={{0,4},{4,0},{8,12},{12,8},{16,20},{20,16},{24,28},{28,24},{1,5},{5... | collective-permute-start | bytes 196616 | tf_op jit(solution)/shard_map/ppermute | solution.py:152
  17.8 3.4 %collective-permute-start.6 = (f32[16,256]{1,0:T(8,128)S(1)}, f32[16,256]{1,0:T(8,128)S(1)}, u32[]{:S(2)}, u32[]{:S(2)}) collective-permute-start(f32[16,256]{1,0:T(8,128)S(1)} %low.1.low0_ref), channel_id=1, source_target_pairs={{0,3},{1,2},{2,1},{3,0},{4,7},{5,6},{6,5},{7,4},{8,11},{9,10},{10,... | collective-permute-start | bytes 49160 | tf_op jit(solution)/shard_map/ppermute | solution.py:152
  17.9 3.8 %collective-permute-start.7 = (f32[16,256]{1,0:T(8,128)S(1)}, f32[16,256]{1,0:T(8,128)S(1)}, u32[]{:S(2)}, u32[]{:S(2)}) collective-permute-start(f32[16,256]{1,0:T(8,128)S(1)} %low.1.low0_ref), channel_id=1, source_target_pairs={{0,2},{1,3},{2,0},{3,1},{4,6},{5,7},{6,4},{7,5},{8,10},{9,11},{10,... | collective-permute-start | bytes 49160 | tf_op jit(solution)/shard_map/ppermute | solution.py:152
  19.4 2.3 %collective-permute-start.8 = (f32[16,256]{1,0:T(8,128)S(1)}, f32[16,256]{1,0:T(8,128)S(1)}, u32[]{:S(2)}, u32[]{:S(2)}) collective-permute-start(f32[16,256]{1,0:T(8,128)S(1)} %low.1.low0_ref), channel_id=1, source_target_pairs={{0,1},{1,0},{2,3},{3,2},{4,5},{5,4},{6,7},{7,6},{8,9},{9,8},{10,11... | collective-permute-start | bytes 49160 | tf_op jit(solution)/shard_map/ppermute | solution.py:152
